TPU v7x, 256 devices: a whole 4x4x8 slice. The times are simulated.
256 devices in a mesh: acq: 32 (over z, y), az: 8 (over x, core).
Axes of the slice: x: 4, y: 4, z: 8, core: 2. Of those that a mesh axis runs over, the one named last changes fastest.
Arguments:
- slc_re: float32 [192, 80, 1280], P('acq', 'az')
- slc_im: float32 [192, 80, 1280], P('acq', 'az')
- pairs: int32 [512, 2], P('acq'), may hold values from 0 to 191, as said below
Outputs:
- coherence: float32 [512, 16, 64], P('acq', 'az')
- ifg_re: float32 [512, 16, 64], P('acq', 'az')
- ifg_im: float32 [512, 16, 64], P('acq', 'az')
Inputs may be any that keep to these rules, and one draw needn't show every extreme that they name: `pairs`: rows d * 16 to (d + 1) * 16 - 1 have their reference acquisition among d * 6 to (d + 1) * 6 - 1. Within such a block of rows, the secondaries taken from any one aligned group of 6 acquisitions are all the same acquisition. A pair's two acquisitions differ.
All inputs are finite; a program needn't handle non-finite values.
Results may differ from a plain program's by a relative error of at most 0.00002.
Values sent between devices are 32-bit elements; how exact they have to be, the bound alone decides.
No kernel may reach another device: no remote copies, remote signals or barrier semaphores. Data moves between devices by JAX's collectives and lax.ppermute only.
A program may use at most 128 MiB of HBM per device.

v0:
```python
import jax
import jax.numpy as jnp
from jax import lax
from jax.sharding import PartitionSpec as P


def padded_2(cells, sides, width):
    for axis, dim in sides:
        count = lax.axis_size(axis)
        ends = count - 1
        head = lax.slice_in_dim(cells, 0, width, axis=dim)
        tail = lax.slice_in_dim(cells, cells.shape[dim] - width, cells.shape[dim], axis=dim)
        cells = jnp.concatenate(
            [
                lax.ppermute(tail, axis, [(i, (i + 1) % count) for i in range(ends)]),
                cells,
                lax.ppermute(head, axis, [((i + 1) % count, i) for i in range(ends)]),
            ],
            axis=dim,
        )
    return cells


def cross_terms(anchor, partner):
    anchor_re = anchor[..., 0, :, :]
    anchor_im = anchor[..., 1, :, :]
    partner_re = partner[..., 0, :, :]
    partner_im = partner[..., 1, :, :]
    return jnp.stack(
        [
            anchor_re * partner_re + anchor_im * partner_im,
            anchor_im * partner_re - anchor_re * partner_im,
            anchor_re * anchor_re + anchor_im * anchor_im,
            partner_re * partner_re + partner_im * partner_im,
        ],
        axis=-3,
    )


def range_box(values):
    width = values.shape[-1]
    padded = jnp.pad(values, [(0, 0)] * (values.ndim - 1) + [(10, 9)])
    sum_two = padded[..., :-1] + padded[..., 1:]
    sum_four = sum_two[..., :-2] + sum_two[..., 2:]
    sum_eight = sum_four[..., :-4] + sum_four[..., 4:]
    sum_sixteen = sum_eight[..., :-8] + sum_eight[..., 8:]
    return sum_sixteen[..., :width] + sum_four[..., 16 : 16 + width]


def azimuth_box(values, height):
    summed = values[..., 0:height, :]
    for offset in range(1, 5):
        summed = summed + values[..., offset : offset + height, :]
    return summed


def look_sum(values):
    height = values.shape[-2]
    width = values.shape[-1]
    shaped = values.reshape(values.shape[:-2] + (height // 5, 5, width // 20, 20))
    return jnp.sum(shaped, axis=(-3, -1))


def finish(direct, window):
    magnitude = jnp.sqrt(window[..., 0, :, :] ** 2 + window[..., 1, :, :] ** 2)
    local_coh = magnitude / jnp.sqrt(window[..., 2, :, :] * window[..., 3, :, :] + 1e-06)
    coherence = look_sum(local_coh) / 100.0
    looked = look_sum(direct)
    scale_look = jnp.sqrt(looked[..., 2, :, :] * looked[..., 3, :, :] + 1e-06)
    return (coherence, looked[..., 0, :, :] / scale_look, looked[..., 1, :, :] / scale_look)


def per_device(slc_re, slc_im, pairs):
    acq_dev = slc_re.shape[0]
    height = slc_re.shape[1]
    devices = lax.axis_size("acq")
    acq_tiles = jnp.stack([slc_re, slc_im], axis=1)
    first_local = pairs[:, 0] % acq_dev
    second = pairs[:, 1]
    source = second // acq_dev
    second_local = second % acq_dev
    matches = source[None, :] == jnp.arange(devices, dtype=jnp.int32)[:, None]
    wanted = jnp.max(jnp.where(matches, second_local[None, :], 0), axis=1)
    requested = lax.all_to_all(wanted[:, None], "acq", split_axis=0, concat_axis=0, tiled=True)[
        :, 0
    ]
    outgoing = acq_tiles[requested]
    incoming = lax.all_to_all(outgoing, "acq", split_axis=0, concat_axis=0, tiled=True)
    partner = incoming[source]
    anchor = acq_tiles[first_local]
    direct = cross_terms(anchor, partner)
    ranged = range_box(direct)
    padded = padded_2(ranged, (("az", 2),), 2)
    window = azimuth_box(padded, height)
    coherence, ifg_re, ifg_im = finish(direct, window)
    return (coherence, ifg_re, ifg_im)


def solution(mesh):
    in_specs = (P("acq", "az", None), P("acq", "az", None), P("acq", None))
    out_specs = (P("acq", "az", None), P("acq", "az", None), P("acq", "az", None))
    return jax.shard_map(
        per_device, mesh=mesh, in_specs=in_specs, out_specs=out_specs, check_vma=False
    )
```

profile of v0, /device:TPU:1, one launch (start us, length us, event | category | flops | bytes accessed | tf_op | source)
XLA Modules:
  0.0 196.5 jit_solution(17475812568577206119)
XLA Ops:
  2.9 12.0 %all-to-all-start = ((s32[32,1,1]{2,1,0:T(1,128)}), s32[32,1,1]{2,1,0:T(1,128)S(1)}, u32[]{:S(2)}, u32[]{:S(2)}) async-start(s32[32,1,1]{2,1,0:T(1,128)} %copy.66), calls=%async_computation | async-start | bytes 32768 | tf_op jit(solution)/shard_map/all_to_all | solution.py:84
  18.1 5.3 %all-to-all-done = s32[32,1,1]{2,1,0:T(1,128)S(1)} async-done(((s32[32,1,1]{2,1,0:T(1,128)}), s32[32,1,1]{2,1,0:T(1,128)S(1)}, u32[]{:S(2)}, u32[]{:S(2)}) %all-to-all-start) | async-done | bytes 160 | tf_op jit(solution)/shard_map/all_to_all | solution.py:84
  24.1 5.6 %gather_fusion.1 = f32[32,2,10,1280]{3,1,2,0:T(2,128)} fusion(f32[6,2,10,1280]{3,1,2,0:T(2,128)S(1)} %pad_maximum_fusion.2, s32[1024]{0:T(1024)S(1)} %pad_clamp_fusion.1), kind=kCustom, calls=%fused_computation.1 | custom fusion | bytes 6553728 | tf_op jit(solution)/shard_map/gather | solution.py:87
  29.8 5.0 %all-to-all-start.1 = ((f32[32,2,10,1280]{3,1,2,0:T(2,128)}), f32[32,2,10,1280]{3,1,2,0:T(2,128)}, u32[]{:S(2)}, u32[]{:S(2)}) async-start(f32[32,2,10,1280]{3,1,2,0:T(2,128)} %gather_fusion.1), calls=%async_computation.1 | async-start | bytes 6553600 | tf_op jit(solution)/shard_map/all_to_all | solution.py:88
  34.8 2.4 %gather_fusion = f32[16,2,10,1280]{3,1,2,0:T(2,128)S(1)} fusion(f32[6,2,10,1280]{3,1,2,0:T(2,128)S(1)} %pad_maximum_fusion.2, s32[1024]{0:T(1024)S(1)} %pad_clamp_fusion.2), kind=kCustom, calls=%fused_computation | custom fusion | bytes 3276864 | tf_op jit(solution)/shard_map/gather | solution.py:90
  37.2 2.5 %fusion.22 = (f32[16,1,10,1280]{3,1,2,0:T(1,128)}, f32[16,1,10,1280]{3,1,2,0:T(1,128)}) fusion(f32[16,2,10,1280]{3,1,2,0:T(2,128)S(1)} %gather_fusion), kind=kLoop, calls=%fused_computation.68 | loop fusion | bytes 3276800 | tf_op jit(solution)/shard_map/slice | solution.py:25
  39.6 68.5 %all-to-all-done.1 = f32[32,2,10,1280]{3,1,2,0:T(2,128)} async-done(((f32[32,2,10,1280]{3,1,2,0:T(2,128)}), f32[32,2,10,1280]{3,1,2,0:T(2,128)}, u32[]{:S(2)}, u32[]{:S(2)}) %all-to-all-start.1) | async-done | bytes 3276832 | tf_op jit(solution)/shard_map/all_to_all | solution.py:88
  108.1 4.3 %gather_fusion.2 = f32[16,2,10,1280]{3,1,2,0:T(2,128)S(1)} fusion(f32[32,2,10,1280]{3,1,2,0:T(2,128)} %all-to-all-done.1, s32[1024]{0:T(1024)S(1)} %pad_clamp_fusion), kind=kCustom, calls=%fused_computation.2 | custom fusion | bytes 3276864 | tf_op jit(solution)/shard_map/gather | solution.py:89
  114.3 7.7 %stack.30 = f32[16,1,2,5,64,20]{5,4,0,3,2,1:T(8,128)} reshape(f32[16,1,10,1280]{3,0,2,1:T(8,128)S(1)} %get-tuple-element.21) | data formatting | bytes 1638400 | tf_op jit(solution)/shard_map/stack | solution.py:29
  122.0 7.7 %stack.31 = f32[16,1,2,5,64,20]{5,4,0,3,2,1:T(8,128)} reshape(f32[16,1,10,1280]{3,0,2,1:T(8,128)S(1)} %get-tuple-element.22) | data formatting | bytes 1638400 | tf_op jit(solution)/shard_map/stack | solution.py:29
  129.7 7.6 %stack.32 = f32[16,1,2,5,64,20]{5,4,0,3,2,1:T(8,128)} reshape(f32[16,1,10,1280]{3,0,2,1:T(8,128)S(1)} %get-tuple-element.23) | data formatting | bytes 1638400 | tf_op jit(solution)/shard_map/stack | solution.py:29
  137.3 2.7 %select_maximum_fusion = f32[16,4,10,1299]{3,0,2,1:T(8,128)} fusion(f32[16,1,10,1280]{3,0,2,1:T(8,128)S(1)} %get-tuple-element.24, f32[16,1,10,1280]{3,0,2,1:T(8,128)S(1)} %get-tuple-element.23, f32[16,1,10,1280]{3,0,2,1:T(8,128)S(1)} %get-tuple-element.22, f32[16,1,10,1280]{3,0,2,1:T(8,128)S(1)} %get-tuple-element.21), kind=kLoop, calls=%fused_computation.13 | loop fusion | flops 8313600 | bytes 6602240 | tf_op jit(solution)/shard_map/stack | solution.py:29
  140.0 7.6 %stack.33 = f32[16,1,2,5,64,20]{5,4,0,3,2,1:T(8,128)} reshape(f32[16,1,10,1280]{3,0,2,1:T(8,128)S(1)} %get-tuple-element.24) | data formatting | bytes 1638400 | tf_op jit(solution)/shard_map/stack | solution.py:29
  147.6 4.1 %slice_add_fusion.2 = f32[16,4,10,1298]{3,0,2,1:T(8,128)S(1)} fusion(f32[16,4,10,1299]{3,0,2,1:T(8,128)} %select_maximum_fusion), kind=kLoop, calls=%fused_computation.12 | loop fusion | flops 830720 | bytes 9968640 | tf_op jit(solution)/shard_map/add | solution.py:43
  153.8 4.6 %fusion.20 = (f32[16,4,10,1284]{3,0,2,1:T(8,128)}, f32[16,4,10,1284]{3,0,2,1:T(8,128)}) fusion(f32[16,4,10,1292]{3,0,2,1:T(8,128)S(1)} %slice_add_fusion), kind=kLoop, calls=%fused_computation.66 | loop fusion | bytes 13148160 | tf_op jit(solution)/shard_map/slice | solution.py:46
  158.4 5.8 %slice_add_fusion.3 = f32[16,4,10,1280]{3,0,2,1:T(8,128)} fusion(f32[16,4,10,1296]{3,0,2,1:T(8,128)S(1)} %slice_add_fusion.1, f32[16,4,10,1284]{3,0,2,1:T(8,128)} %get-tuple-element.18, f32[16,4,10,1284]{3,0,2,1:T(8,128)} %get-tuple-element.17), kind=kLoop, calls=%fused_computation.25 | loop fusion | flops 1638400 | bytes 13107200 | tf_op jit(solution)/shard_map/add | solution.py:47
  164.2 1.7 fusion.21
  165.9 5.4 %collective-permute-start = (f32[16,4,2,1280]{3,0,2,1:T(8,128)S(1)}, f32[16,4,2,1280]{3,0,2,1:T(8,128)S(1)}, u32[]{:S(2)}, u32[]{:S(2)}) collective-permute-start(f32[16,4,2,1280]{3,0,2,1:T(8,128)S(1)} %get-tuple-element.19), channel_id=1, source_target_pairs={{0,1},{1,2},{2,3},{3,4},{4,5},{5,6},{6,7},{8,9},{9,10},{10,11},{11... | collective-permute-start | bytes 1966088 | tf_op jit(solution)/shard_map/ppermute | solution.py:15
  171.3 2.2 %collective-permute-start.1 = (f32[16,4,2,1280]{3,0,2,1:T(8,128)S(1)}, f32[16,4,2,1280]{3,0,2,1:T(8,128)S(1)}, u32[]{:S(2)}, u32[]{:S(2)}) collective-permute-start(f32[16,4,2,1280]{3,0,2,1:T(8,128)S(1)} %get-tuple-element.20), channel_id=1, source_target_pairs={{1,0},{2,1},{3,2},{4,3},{5,4},{6,5},{7,6},{9,8},{10,9},{11,10},{12... | collective-permute-start | bytes 1966088 | tf_op jit(solution)/shard_map/ppermute | solution.py:17
  173.6 6.1 %maximum_reduce_fusion = f32[16,4,2,64]{3,0,2,1:T(8,128)S(1)} fusion(f32[16,1,2,5,64,20]{5,4,0,3,2,1:T(8,128)S(1)} %bitcast.51, f32[16,1,2,5,64,20]{5,4,0,3,2,1:T(8,128)S(1)} %bitcast.49, f32[16,1,2,5,64,20]{5,4,0,3,2,1:T(8,128)S(1)} %bitcast.47, f32[16,1,2,5,64,20]{5,4,0,3,2,1:T(8,128)S(1)} %bitcast.45), kind=kLoop, calls=%fused_computation.3 | loop fusion | flops 3268608 | bytes 3309568 | tf_op jit(solution)/shard_map/reduce_sum | solution.py:61
  181.0 2.5 %collective-permute-done.1 = f32[16,4,2,1280]{3,0,2,1:T(8,128)S(1)} collective-permute-done((f32[16,4,2,1280]{3,0,2,1:T(8,128)S(1)}, f32[16,4,2,1280]{3,0,2,1:T(8,128)S(1)}, u32[]{:S(2)}, u32[]{:S(2)}) %collective-permute-start.1) | collective-permute-done | bytes 655392 | tf_op jit(solution)/shard_map/ppermute | solution.py:17
  183.5 1.4 fusion.3
  185.3 7.7 %div.40 = f32[16,2,5,64,20]{4,3,0,2,1:T(8,128)} reshape(f32[16,1,10,1280]{3,0,2,1:T(8,128)S(1)} %fusion.9) | data formatting | bytes 1638400 | tf_op jit(solution)/shard_map/div | solution.py:66
  193.0 2.9 %reduce_sum.18 = f32[16,2,64]{2,0,1:T(8,128)S(1)} reduce(f32[16,2,5,64,20]{4,3,0,2,1:T(8,128)} %div.40, f32[]{:T(128)} %constant.38.clone.1), dimensions={2,4}, to_apply=%region_1.2 | reduce | flops 202752 | bytes 827396 | tf_op jit(solution)/shard_map/reduce_sum | solution.py:61
  (49 shorter events, 12.3 us)
Async XLA Ops:
  2.9 20.6 %all-to-all-start = ((s32[32,1,1]{2,1,0:T(1,128)}), s32[32,1,1]{2,1,0:T(1,128)S(1)}, u32[]{:S(2)}, u32[]{:S(2)}) async-start(s32[32,1,1]{2,1,0:T(1,128)} %copy.66), calls=%async_computation | async-start | bytes 32768 | tf_op jit(solution)/shard_map/all_to_all | solution.py:84
  29.8 78.3 %all-to-all-start.1 = ((f32[32,2,10,1280]{3,1,2,0:T(2,128)}), f32[32,2,10,1280]{3,1,2,0:T(2,128)}, u32[]{:S(2)}, u32[]{:S(2)}) async-start(f32[32,2,10,1280]{3,1,2,0:T(2,128)} %gather_fusion.1), calls=%async_computation.1 | async-start | bytes 6553600 | tf_op jit(solution)/shard_map/all_to_all | solution.py:88
  112.4 1.3 copy-start.1
  112.4 1.4 copy-start.2
  152.7 20.8 %slice-start.4 = ((s8[5242880]{0:T(1024)(128)(4,1)}), s8[4194304]{0:T(1024)(128)(4,1)S(1)}, s32[]{:S(2)}) async-start(s8[5242880]{0:T(1024)(128)(4,1)} %bitcast.48), calls=%async_computation.6 | async-start | bytes 8388608
  152.7 20.8 %slice-start.6 = ((s8[5242880]{0:T(1024)(128)(4,1)}), s8[4194304]{0:T(1024)(128)(4,1)S(1)}, s32[]{:S(2)}) async-start(s8[5242880]{0:T(1024)(128)(4,1)} %bitcast.50), calls=%async_computation.8 | async-start | bytes 8388608
  153.8 19.8 %slice-start.5 = ((s8[5242880]{0:T(1024)(128)(4,1)}), s8[1048576]{0:T(1024)(128)(4,1)S(1)}, s32[]{:S(2)}) async-start(s8[5242880]{0:T(1024)(128)(4,1)} %bitcast.48), calls=%async_computation.7 | async-start | bytes 2097152
  153.8 19.8 %slice-start.7 = ((s8[5242880]{0:T(1024)(128)(4,1)}), s8[1048576]{0:T(1024)(128)(4,1)S(1)}, s32[]{:S(2)}) async-start(s8[5242880]{0:T(1024)(128)(4,1)} %bitcast.50), calls=%async_computation.9 | async-start | bytes 2097152
  158.3 15.2 %slice-start = ((s8[5242880]{0:T(1024)(128)(4,1)}), s8[4194304]{0:T(1024)(128)(4,1)S(1)}, s32[]{:S(2)}) async-start(s8[5242880]{0:T(1024)(128)(4,1)} %bitcast.44), calls=%async_computation.2 | async-start | bytes 8388608
  158.3 15.2 %slice-start.2 = ((s8[5242880]{0:T(1024)(128)(4,1)}), s8[4194304]{0:T(1024)(128)(4,1)S(1)}, s32[]{:S(2)}) async-start(s8[5242880]{0:T(1024)(128)(4,1)} %bitcast.46), calls=%async_computation.4 | async-start | bytes 8388608
  158.3 15.2 %slice-start.1 = ((s8[5242880]{0:T(1024)(128)(4,1)}), s8[1048576]{0:T(1024)(128)(4,1)S(1)}, s32[]{:S(2)}) async-start(s8[5242880]{0:T(1024)(128)(4,1)} %bitcast.44), calls=%async_computation.3 | async-start | bytes 2097152
  158.4 15.2 %slice-start.3 = ((s8[5242880]{0:T(1024)(128)(4,1)}), s8[1048576]{0:T(1024)(128)(4,1)S(1)}, s32[]{:S(2)}) async-start(s8[5242880]{0:T(1024)(128)(4,1)} %bitcast.46), calls=%async_computation.5 | async-start | bytes 2097152
  165.9 15.1 %collective-permute-start = (f32[16,4,2,1280]{3,0,2,1:T(8,128)S(1)}, f32[16,4,2,1280]{3,0,2,1:T(8,128)S(1)}, u32[]{:S(2)}, u32[]{:S(2)}) collective-permute-start(f32[16,4,2,1280]{3,0,2,1:T(8,128)S(1)} %get-tuple-element.19), channel_id=1, source_target_pairs={{0,1},{1,2},{2,3},{3,4},{4,5},{5,6},{6,7},{8,9},{9,10},{10,11},{11... | collective-permute-start | bytes 1966088 | tf_op jit(solution)/shard_map/ppermute | solution.py:15
  171.3 12.2 %copy-start = (f32[16,4,10,1280]{3,0,2,1:T(8,128)S(1)}, f32[16,4,10,1280]{3,0,2,1:T(8,128)}, u32[]{:S(2)}) copy-start(f32[16,4,10,1280]{3,0,2,1:T(8,128)} %slice_add_fusion.3) | copy-start | bytes 9830404
  171.3 12.2 %collective-permute-start.1 = (f32[16,4,2,1280]{3,0,2,1:T(8,128)S(1)}, f32[16,4,2,1280]{3,0,2,1:T(8,128)S(1)}, u32[]{:S(2)}, u32[]{:S(2)}) collective-permute-start(f32[16,4,2,1280]{3,0,2,1:T(8,128)S(1)} %get-tuple-element.20), channel_id=1, source_target_pairs={{1,0},{2,1},{3,2},{4,3},{5,4},{6,5},{7,6},{9,8},{10,9},{11,10},{12... | collective-permute-start | bytes 1966088 | tf_op jit(solution)/shard_map/ppermute | solution.py:17
where the time goes:
time: 197 us; the launch traced here: 196 us
  waiting for transfers between devices  76.3 us (39%)
  local copies, waits for them, and re-layouts  65.8 us (33%)
  other arithmetic  28.8 us (15%)
  starting transfers between devices  24.6 us (12%)
    all_to_all x1, waiting for transfers between devices, per_device(): lax.all_to_all(outgoing, 'acq', split_axis=0, concat_axis=0, tiled=True)  68.5 us
    another operation x4, local copies, waits for them, and re-layouts, cross_terms(): jnp.stack([anchor_re * partner_re + anchor_im * partner_im, anchor_im * p...  30.6 us
    all_to_all x1, starting transfers between devices, per_device(): lax.all_to_all(wanted[:, None], 'acq', split_axis=0, concat_axis=0, tiled...  12 us
    reduce_sum x2, other arithmetic, look_sum(): return jnp.sum(shaped, axis=(-3, -1))  8.97 us
    div x1, local copies, waits for them, and re-layouts, finish(): magnitude / jnp.sqrt(window[..., 2, :, :] * window[..., 3, :, :] + 1e-06)  7.67 us
    add x1, other arithmetic, range_box(): return sum_sixteen[..., :width] + sum_four[..., 16:16 + width]  5.85 us
    gather x1, local copies, waits for them, and re-layouts, per_device(): outgoing = acq_tiles[requested]  5.64 us
    ppermute x1, starting transfers between devices, padded_2(): lax.ppermute(tail, axis, [(i, (i + 1) % count) for i in range(ends)])  5.4 us
  transfers between devices with their start and end apart: 4, of which 3 were waited for; matrix products, arithmetic and copies ran while one was open for 8% of the time, Pallas kernels for 0%

commit v1 on v0

v1 whole, which is shorter than its diff:
```python
import jax
import jax.numpy as jnp
from jax import lax
from jax.experimental import pallas as pl
from jax.experimental.pallas import tpu as pltpu
from jax.sharding import PartitionSpec as P

DEVS = 32
ACQ_DEV = 6
ACQ = DEVS * ACQ_DEV
PAIR_DEV = 16
PAIRS = DEVS * PAIR_DEV
ROWS = 10
HALF = 5
RG = 1280
STEP = 40
WIDE = STEP + 19
CHUNK = 60
K = 256
F32 = jnp.float32
BF16 = jnp.bfloat16
VMEM = pl.BlockSpec(memory_space=pltpu.VMEM)
HBM = pl.BlockSpec(memory_space=pltpu.HBM)
BIG = 3.38e38
PART = 8 * ACQ_DEV


def lanes_of(shape):
    return lax.broadcasted_iota(jnp.int32, shape, len(shape) - 1)


def pack_kernel(re_hbm, im_hbm, pairs_hbm, out_ref, re_ref, im_ref, pairs_ref, sems):
    copies = [
        pltpu.make_async_copy(source, target, sems.at[n])
        for n, (source, target) in enumerate(((pairs_hbm, pairs_ref), (re_hbm, re_ref), (im_hbm, im_ref)))
    ]
    for copy in copies:
        copy.start()
    lane = lanes_of((ACQ_DEV, 128))
    wide = lanes_of((PAIR_DEV, 128))
    copies[0].wait()
    acq = pairs_ref[...]
    group = (acq * 171) >> 10
    local = (acq - ACQ_DEV * group) * 8 + (group & 7)
    order = lax.broadcasted_iota(jnp.int32, (2, PAIR_DEV), 0)
    index = (local + jnp.where(order == 0, 0, (group >> 3) * PART)).astype(F32)
    square = (PAIR_DEV, PAIR_DEV)
    diagonal = lax.broadcasted_iota(jnp.int32, square, 0) == lax.broadcasted_iota(jnp.int32, square, 1)
    columns = [
        jnp.sum(jnp.where(diagonal, jnp.broadcast_to(index[w : w + 1, :], square), 0.0), axis=1, keepdims=True)
        for w in range(2)
    ]
    first, second = [jnp.broadcast_to(column, (PAIR_DEV, 128)) for column in columns]
    for part, ref in enumerate((re_ref, im_ref)):
        copies[1 + part].wait()
        for r in range(HALF):
            for d in range(DEVS):
                start = STEP * d - 10
                k = start // 128
                off = start - 128 * k
                halves = []
                for row, base in ((r, 0), (r + HALF, 64)):
                    shift = (base - off) % 128
                    pieces = []
                    for t in (k, k + 1):
                        if 0 <= t < RG // 128 and (t == k or off + WIDE > 128):
                            x = ref[row, :, t * 128 : (t + 1) * 128]
                            pieces.append(pltpu.roll(x, shift, 1) if shift else x)
                        else:
                            pieces.append(jnp.zeros((ACQ_DEV, 128), F32))
                    if off + WIDE > 128:
                        halves.append(jnp.where(lane < base + 128 - off, pieces[0], pieces[1]))
                    else:
                        halves.append(pieces[0])
                top = d * CHUNK + (part * HALF + r) * ACQ_DEV
                both = jnp.where(lane < 64, halves[0], halves[1])
                out_ref[top : top + ACQ_DEV, :] = jnp.where((lane & 63) < WIDE, both, 0.0)
    for d in range(DEVS):
        head = out_ref[d * CHUNK : d * CHUNK + PAIR_DEV, :]
        head = jnp.where(wide == 60, first, jnp.where(wide == 61, second, head))
        out_ref[d * CHUNK : d * CHUNK + PAIR_DEV, :] = head


def acq_rows(recv_ref, part, r):
    base = (part * HALF + r) * ACQ_DEV
    return jnp.concatenate(
        [recv_ref[pl.ds(base + a + 8 * g * CHUNK, 8, stride=CHUNK), :] for g in range(4) for a in range(ACQ_DEV)],
        axis=0,
    )


def edges_kernel(recv_ref, low_ref, high_ref):
    lane = lanes_of((ACQ, 128))
    for part in range(2):
        rows = [acq_rows(recv_ref, part, r) for r in (0, 1, 3, 4)]
        low_ref[part * ACQ : (part + 1) * ACQ, :] = jnp.where(lane < 64, rows[0], pltpu.roll(rows[1], 64, 1))
        high_ref[part * ACQ : (part + 1) * ACQ, :] = jnp.where(lane < 64, pltpu.roll(rows[2], 64, 1), rows[3])


def pieces_of(x, count):
    out = []
    for n in range(count):
        piece = x.astype(BF16)
        out.append(piece)
        if n + 1 < count:
            x = x - piece.astype(F32)
    return out


def clamp(x):
    return jnp.minimum(jnp.maximum(x, -BIG), BIG)


def dot(x, y):
    return jnp.dot(x, y, preferred_element_type=F32)


def fill(table):
    for p in range(3):
        table[p * K + ACQ : (p + 1) * K, :] = jnp.zeros((K - ACQ, table.shape[1]), BF16)


def enter(table, x, at):
    for p, piece in enumerate(pieces_of(clamp(x), 3)):
        table[p * K : p * K + ACQ, at : at + x.shape[1]] = piece


def along_range():
    shape = (128, 128)
    k = lax.broadcasted_iota(jnp.int32, shape, 0)
    n = lax.broadcasted_iota(jnp.int32, shape, 1)
    c = n & 63
    first = jnp.where(c < STEP, c, jnp.where(c < STEP + 4, 10 + 20 * (c & 1), -1000))
    sample = k & 63
    inside = ((k >> 6) == (n >> 6)) & (sample >= first) & (sample <= first + 19)
    box = jnp.where(inside, 1.0, 0.0).astype(BF16)
    return jnp.concatenate([box, box], axis=0)


def choose(pick_a, pick_b, table, picked, at, width):
    columns = slice(at, at + width)
    picked[PAIRS:, columns] = dot(pick_b[...], table[:, columns])
    for g in range(4):
        few = jnp.concatenate([table[p * K + g * PART : p * K + (g + 1) * PART, columns] for p in range(3)], axis=0)
        picked[128 * g : 128 * (g + 1), columns] = dot(pick_a[128 * g : 128 * (g + 1), : 3 * PART], few)


def cross(picked, top, count):
    fields = [[], []]
    for t in range(count):
        ra = picked[pl.ds(top, 16), t * 256 : t * 256 + 128]
        ia = picked[pl.ds(top, 16), t * 256 + 128 : t * 256 + 256]
        rb = picked[pl.ds(top + PAIRS, 16), t * 256 : t * 256 + 128]
        ib = picked[pl.ds(top + PAIRS, 16), t * 256 + 128 : t * 256 + 256]
        fields[0].append(ra * rb + ia * ib)
        fields[1].append(ia * rb - ra * ib)
    return fields


def own_rows(v):
    v0, v1, v2, v3, v4 = v
    low = lanes_of(v0.shape) < 64
    v12, v34 = v1 + v2, v3 + v4
    v012, v234 = v0 + v12, v2 + v34
    return [
        v012 + jnp.where(low, 0.0, pltpu.roll(v34, 64, 1)),
        (v012 + v3) + jnp.where(low, 0.0, pltpu.roll(v4, 64, 1)),
        v012 + v34,
        (v1 + v234) + jnp.where(low, pltpu.roll(v0, 64, 1), 0.0),
        v234 + jnp.where(low, pltpu.roll(v0 + v1, 64, 1), 0.0),
    ]


def edge_rows(v, up, down):
    low = lanes_of(up.shape) < 64
    up_turned, down_turned = pltpu.roll(up, 64, 1), pltpu.roll(down, 64, 1)
    return [
        v[0] + jnp.where(low, up + up_turned, 0.0),
        v[1] + jnp.where(low, up_turned, 0.0),
        v[2],
        v[3] + jnp.where(low, 0.0, down_turned),
        v[4] + jnp.where(low, 0.0, down + down_turned),
    ]


def own_kernel(recv_ref, sums_ref, power_ref, pick_a, pick_b, table, picked):
    lane = lanes_of((128, K))
    few = lane - PART * ((lane * 342) >> 14)
    for g in range(4):
        head = jnp.concatenate([recv_ref[pl.ds(8 * g * CHUNK + p, 8, stride=CHUNK), :] for p in range(PAIR_DEV)], axis=0)
        rows = slice(128 * g, 128 * (g + 1))
        index = jnp.broadcast_to(head[:, 60:61], (128, K))
        pick_a[rows, :] = jnp.where(index == few.astype(F32), 1.0, 0.0).astype(BF16)
        index = jnp.broadcast_to(head[:, 61:62], (128, K))
        hot = jnp.where(index == lane.astype(F32), 1.0, 0.0).astype(BF16)
        for p in range(3):
            pick_b[rows, p * K : (p + 1) * K] = hot
    fill(table)
    squares = []
    for t in range(HALF):
        parts = [acq_rows(recv_ref, part, t) for part in range(2)]
        for part, x in enumerate(parts):
            enter(table, x, t * 256 + part * 128)
        squares.append(parts[0] * parts[0] + parts[1] * parts[1])
        choose(pick_a, pick_b, table, picked, t * 256, 256)
    for r, x in enumerate(own_rows(squares)):
        power_ref[:, r * 128 : (r + 1) * 128] = x

    def some(g, carry):
        top = pl.multiple_of(16 * g, 16)
        for f, field in enumerate(cross(picked, top, HALF)):
            for r, x in enumerate(own_rows(field)):
                sums_ref[pl.ds(top + f * PAIRS, 16), r * 128 : (r + 1) * 128] = x
        return carry

    lax.fori_loop(0, PAIRS // 16, some, 0, unroll=True)


def pair_kernel(up_ref, down_ref, sums_ref, power_ref, pick_a, pick_b, out_ref, table, picked, terms, total, ends):
    fill(table)
    box = along_range()
    squares = []
    for t, ref in enumerate((up_ref, down_ref)):
        parts = [ref[part * ACQ : (part + 1) * ACQ, :] for part in range(2)]
        for part, x in enumerate(parts):
            enter(table, x, t * 256 + part * 128)
        squares.append(parts[0] * parts[0] + parts[1] * parts[1])
        choose(pick_a, pick_b, table, picked, t * 256, 256)
    own = [power_ref[:, r * 128 : (r + 1) * 128] for r in range(HALF)]
    for r, x in enumerate(edge_rows(own, *squares)):
        enter(table, dot(jnp.concatenate(pieces_of(x, 2), axis=1), box), 512 + r * 128)
    choose(pick_a, pick_b, table, picked, 512, 640)

    def rows(g, carry):
        top = pl.multiple_of(16 * g, 16)
        for f, field in enumerate(cross(picked, top, 2)):
            own = [sums_ref[pl.ds(top + f * PAIRS, 16), r * 128 : (r + 1) * 128] for r in range(HALF)]
            for r, x in enumerate(edge_rows(own, *field)):
                for n, piece in enumerate(pieces_of(x, 2)):
                    terms[pl.ds(top + (2 * r + f) * PAIRS, 16), n * 128 : (n + 1) * 128] = piece
        return carry

    lax.fori_loop(0, PAIRS // 16, rows, 0, unroll=True)
    total[...] = dot(terms[...], box)

    lane = lanes_of((16, 128)) & 63

    def some(g, carry):
        top = pl.multiple_of(16 * g, 16)
        coherence = None
        for r in range(HALF):
            x0 = total[pl.ds(top + 2 * r * PAIRS, 16), :]
            x1 = total[pl.ds(top + (2 * r + 1) * PAIRS, 16), :]
            wa = picked[pl.ds(top, 16), 512 + r * 128 : 640 + r * 128]
            wb = picked[pl.ds(top + PAIRS, 16), 512 + r * 128 : 640 + r * 128]
            inverse = lax.rsqrt(wa * wb + 1e-06)
            num = x0 * x0 + x1 * x1
            size = num * lax.rsqrt(jnp.maximum(num, 1e-37)) * inverse
            coherence = size if coherence is None else coherence + size
            if r == 2:
                look = jnp.where(lane < STEP + 2, x0, x1) * inverse
        value = jnp.where(lane < STEP, coherence, look)
        for p, piece in enumerate(pieces_of(value, 3)):
            ends[pl.ds(top, 16), p * 128 : (p + 1) * 128] = piece
        return carry

    lax.fori_loop(0, PAIRS // 16, some, 0, unroll=True)

    n = lax.broadcasted_iota(jnp.int32, (128, 256), 0)
    m = lax.broadcasted_iota(jnp.int32, (128, 256), 1)
    c, j, o = n & 63, m >> 7, (m >> 5) & 3
    first = jnp.where(o == 0, 20 * j, jnp.where(o == 3, 1000, STEP - 2 + 2 * o + j))
    last = first + jnp.where(o == 0, 19, 0)
    same = ((n >> 6) == (m & 1)) & (c >= first) & (c <= last)
    spread = jnp.where(same, 1.0, 0.0).astype(BF16)
    result = dot(ends[...], jnp.concatenate([spread] * 3, axis=0))
    owner = (lanes_of((8, 128)) >> 1) & 15
    for j in range(2):
        for g in range(4):
            out = None
            for p in range(PAIR_DEV):
                top = 128 * g + 8 * p
                rows_p = result[top : top + 8, j * 128 : (j + 1) * 128]
                out = rows_p if out is None else jnp.where(owner == p, rows_p, out)
            out_ref[pl.ds(16 * g + j, 8, stride=2), :] = out


def finish_kernel(got_ref, coh_ref, re_ref, im_ref):
    turned = jnp.transpose(got_ref[...])
    coh_ref[...] = turned[0:32] * 0.01
    re_ref[...] = turned[32:64]
    im_ref[...] = turned[64:96]


def call(kernel, outs, specs, scratch=(), limit=40, **more):
    return pl.pallas_call(
        kernel,
        out_shape=outs,
        in_specs=specs,
        out_specs=jax.tree.map(lambda _: VMEM, outs),
        scratch_shapes=[pltpu.VMEM(*x) if isinstance(x, tuple) else x for x in scratch],
        compiler_params=pltpu.CompilerParams(vmem_limit_bytes=limit * 1024 * 1024),
        **more,
    )


def f32(*shape):
    return jax.ShapeDtypeStruct(shape, F32)


def bf16(*shape):
    return jax.ShapeDtypeStruct(shape, BF16)


OWN_OUTS = (f32(2 * PAIRS, HALF * 128), f32(ACQ, HALF * 128), bf16(PAIRS, K), bf16(PAIRS, 3 * K))
OWN_SCRATCH = (((3 * K, HALF * 256), BF16), ((2 * PAIRS, HALF * 256), F32))
PAIR_SCRATCH = (
    ((3 * K, 512 + HALF * 128), BF16),
    ((2 * PAIRS, 512 + HALF * 128), F32),
    ((2 * HALF * PAIRS, 256), BF16),
    ((2 * HALF * PAIRS, 128), F32),
    ((PAIRS, 3 * 128), BF16),
)


def per_device(slc_re, slc_im, pairs):
    send = call(
        pack_kernel,
        f32(DEVS * CHUNK, 128),
        [HBM] * 3,
        (
            ((ROWS, ACQ_DEV, RG), F32),
            ((ROWS, ACQ_DEV, RG), F32),
            ((2, PAIR_DEV), jnp.int32),
            pltpu.SemaphoreType.DMA((3,)),
        ),
        limit=60,
    )(jnp.transpose(slc_re, (1, 0, 2)), jnp.transpose(slc_im, (1, 0, 2)), pairs.T)
    send = send.reshape(DEVS, CHUNK // 4, 4, 128)
    recv = lax.all_to_all(send, "acq", split_axis=0, concat_axis=0, tiled=True)
    recv = recv.reshape(DEVS * CHUNK, 128)
    low, high = call(edges_kernel, (f32(2 * ACQ, 128), f32(2 * ACQ, 128)), [VMEM])(recv)
    ends = lax.axis_size("az") - 1
    up = lax.ppermute(high, "az", [(i, i + 1) for i in range(ends)])
    down = lax.ppermute(low, "az", [(i + 1, i) for i in range(ends)])
    cost = pl.CostEstimate(flops=5 * 10**9, bytes_accessed=10**7, transcendentals=0)
    partial = call(own_kernel, OWN_OUTS, [VMEM], OWN_SCRATCH, cost_estimate=cost)(recv)
    result = call(pair_kernel, f32(2 * DEVS, 128), [VMEM] * 6, PAIR_SCRATCH)(up, down, *partial)
    got = lax.all_to_all(result.reshape(DEVS, 2, 128), "acq", split_axis=0, concat_axis=0, tiled=True)
    outs = call(finish_kernel, (f32(32, 64),) * 3, [VMEM])(got.reshape(2 * DEVS, 128))
    return tuple(x.reshape(PAIR_DEV, 2, 64) for x in outs)


def solution(mesh):
    in_specs = (P("acq", "az", None), P("acq", "az", None), P("acq", None))
    out_specs = (P("acq", "az", None), P("acq", "az", None), P("acq", "az", None))
    return jax.shard_map(per_device, mesh=mesh, in_specs=in_specs, out_specs=out_specs, check_vma=False)
```

time: 197 us -> 71.5 us (0.36)
  waiting for transfers between devices: 76.3 us -> 2.89 us
  local copies, waits for them, and re-layouts: 65.8 us -> 0 us
  blocking collectives: 0 us -> 50.4 us
  other arithmetic: 28.8 us -> 0 us
  starting transfers between devices: 24.6 us -> 7.99 us
  Pallas kernels: 0 us -> 9.29 us
    all_to_all x2 -> x0, waiting for transfers between devices: 73.8 us -> none  [the longest x1 68.5 us: per_device(): lax.all_to_all(outgoing, 'acq', split_axis=0, concat_axis=0, tiled=True)]
    all_to_all x0 -> x2, blocking collectives: none -> 50.4 us  [the longest x1 36.9 us: per_device(): recv = lax.all_to_all(send, 'acq', split_axis=0, concat_axis=0, tiled=True)]
    another operation x6 -> x0, local copies, waits for them, and re-layouts: 33.2 us -> none  [the longest x4 30.6 us: cross_terms(): jnp.stack([anchor_re * partner_re + anchor_im * partner_im, anchor_im * p...]
    all_to_all x2 -> x0, starting transfers between devices: 17 us -> none  [the longest x1 12 us: per_device(): lax.all_to_all(wanted[:, None], 'acq', split_axis=0, concat_axis=0, tiled...]
    add x6 -> x0, other arithmetic: 13.9 us -> none  [the longest x1 5.85 us: range_box(): return sum_sixteen[..., :width] + sum_four[..., 16:16 + width]]
    gather x3 -> x0, local copies, waits for them, and re-layouts: 12.3 us -> none  [the longest x1 5.64 us: per_device(): outgoing = acq_tiles[requested]]
    slice x4 -> x0, local copies, waits for them, and re-layouts: 9.97 us -> none  [the longest x1 4.57 us: range_box(): sum_sixteen = sum_eight[..., :-8] + sum_eight[..., 8:]]
    pallas_call x0 -> x5, Pallas kernels: none -> 9.29 us  [the longest x1 3.16 us: per_device(): call(pair_kernel, f32(2 * DEVS, 128), [VMEM] * 6, PAIR_SCRATCH)]
  transfers between devices with their start and end apart: 4 -> 2, of which waited for: 3 -> 1; matrix products, arithmetic and copies ran while one was open for 8% -> 0% of each run, Pallas kernels for 0% -> 3%
where the time goes in v1:
time: 71.5 us; the launch traced here: 71.2 us
  blocking collectives  50.4 us (70%)
  Pallas kernels  9.29 us (13%)
  starting transfers between devices  7.99 us (11%)
  waiting for transfers between devices  2.89 us (4%)
    all_to_all x1, blocking collectives, per_device(): recv = lax.all_to_all(send, 'acq', split_axis=0, concat_axis=0, tiled=True)  36.9 us
    all_to_all x1, blocking collectives, per_device(): lax.all_to_all(result.reshape(DEVS, 2, 128), 'acq', split_axis=0, concat_...  13.5 us
    ppermute x1, starting transfers between devices, per_device(): up = lax.ppermute(high, 'az', [(i, i + 1) for i in range(ends)])  6.07 us
    pallas_call x1, Pallas kernels, per_device(): call(pair_kernel, f32(2 * DEVS, 128), [VMEM] * 6, PAIR_SCRATCH)  3.16 us
    pallas_call x1, Pallas kernels, per_device(): call(pack_kernel, f32(DEVS * CHUNK, 128), [HBM] * 3, (((ROWS, ACQ_DEV, RG...  3.11 us
    ppermute x1, waiting for transfers between devices, per_device(): down = lax.ppermute(low, 'az', [(i + 1, i) for i in range(ends)])  2.89 us
    pallas_call x1, Pallas kernels, per_device(): call(own_kernel, OWN_OUTS, [VMEM], OWN_SCRATCH, cost_estimate=cost)(recv)  2.16 us
    ppermute x1, starting transfers between devices, per_device(): down = lax.ppermute(low, 'az', [(i + 1, i) for i in range(ends)])  1.92 us
  transfers between devices with their start and end apart: 2, of which 1 were waited for; matrix products, arithmetic and copies ran while one was open for 0% of the time, Pallas kernels for 3%

profile of v1, /device:TPU:1, one launch (start us, length us, event | category | flops | bytes accessed | tf_op | source)
XLA Modules:
  0.0 71.2 jit_solution(12636039117502829852)
XLA Ops:
  0.6 3.1 %shard_map.58 = f32[1920,128]{1,0:T(8,128)} custom-call(f32[10,6,1280]{2,1,0:T(8,128)} %bitcast.15, f32[10,6,1280]{2,1,0:T(8,128)} %bitcast.16, s32[2,16]{1,0:T(2,128)} %bitcast.17), custom_call_target="tpu_custom_call" | custom-call | tf_op jit(solution)/shard_map/pallas_call | solution.py:327
  3.8 36.9 %all_to_all.10 = f32[32,15,4,128]{3,2,1,0:T(4,128)S(1)} all-to-all(f32[32,15,4,128]{3,2,1,0:T(4,128)} %bitcast.14), channel_id=1, replica_groups=mesh['acq'=32,'az'=8] {'acq'}, dimensions={0} | all-to-all | bytes 1966080 | tf_op jit(solution)/shard_map/all_to_all | solution.py:340
  40.6 0.2 shard_map.59
  40.8 6.1 %collective-permute-start = (f32[384,128]{1,0:T(8,128)S(1)}, f32[384,128]{1,0:T(8,128)S(1)}, u32[]{:S(2)}, u32[]{:S(2)}) collective-permute-start(f32[384,128]{1,0:T(8,128)S(1)} %get-tuple-element.12), channel_id=1, source_target_pairs={{0,1},{1,2},{2,3},{3,4},{4,5},{5,6},{6,7},{8,9},{9,10},{10,11},{11... | collective-permute-start | bytes 589832 | tf_op jit(solution)/shard_map/ppermute | solution.py:344
  46.8 1.9 %collective-permute-start.1 = (f32[384,128]{1,0:T(8,128)S(1)}, f32[384,128]{1,0:T(8,128)S(1)}, u32[]{:S(2)}, u32[]{:S(2)}) collective-permute-start(f32[384,128]{1,0:T(8,128)S(1)} %get-tuple-element.13), channel_id=1, source_target_pairs={{1,0},{2,1},{3,2},{4,3},{5,4},{6,5},{7,6},{9,8},{10,9},{11,10},{12... | collective-permute-start | bytes 589832 | tf_op jit(solution)/shard_map/ppermute | solution.py:345
  48.8 2.2 %shard_map.60 = (f32[1024,640]{1,0:T(8,128)S(1)}, f32[192,640]{1,0:T(8,128)S(1)}, bf16[512,256]{1,0:T(8,128)(2,1)S(1)}, bf16[512,768]{1,0:T(8,128)(2,1)S(1)}) custom-call(f32[1920,128]{1,0:T(8,128)S(1)} %bitcast.11), custom_call_target="tpu_custom_call" | custom-call | flops 5000000000 | bytes 10000000 | tf_op jit(solution)/shard_map/pallas_call | solution.py:347
  50.9 0.0 collective-permute-done.up_ref
  51.0 2.9 %collective-permute-done.1.down_ref = f32[384,128]{1,0:T(8,128)S(1)} collective-permute-done((f32[384,128]{1,0:T(8,128)S(1)}, f32[384,128]{1,0:T(8,128)S(1)}, u32[]{:S(2)}, u32[]{:S(2)}) %collective-permute-start.1) | collective-permute-done | bytes 196640 | tf_op jit(solution)/shard_map/ppermute | solution.py:345
  53.8 3.2 %shard_map.61 = f32[64,128]{1,0:T(8,128)S(1)} custom-call(f32[384,128]{1,0:T(8,128)S(1)} %collective-permute-done.up_ref, f32[384,128]{1,0:T(8,128)S(1)} %collective-permute-done.1.down_ref, f32[1024,640]{1,0:T(8,128)S(1)} %get-tuple-element.14.sums_ref, f32[192,640]{1,0:T(8,128)S(1)} %get-tuple-element.15.power_ref, ...), custom_call_target="tpu_custom_call" | custom-call | tf_op jit(solution)/shard_map/pallas_call | solution.py:348
  57.0 13.5 %all_to_all.11 = f32[32,2,128]{2,1,0:T(2,128)S(1)} all-to-all(f32[32,2,128]{2,1,0:T(2,128)S(1)} %bitcast.12), channel_id=1, replica_groups=mesh['acq'=32,'az'=8] {'acq'}, dimensions={0} | all-to-all | bytes 65536 | tf_op jit(solution)/shard_map/all_to_all | solution.py:349
  70.5 0.7 shard_map.62
Async XLA Ops:
  40.8 10.2 %collective-permute-start = (f32[384,128]{1,0:T(8,128)S(1)}, f32[384,128]{1,0:T(8,128)S(1)}, u32[]{:S(2)}, u32[]{:S(2)}) collective-permute-start(f32[384,128]{1,0:T(8,128)S(1)} %get-tuple-element.12), channel_id=1, source_target_pairs={{0,1},{1,2},{2,3},{3,4},{4,5},{5,6},{6,7},{8,9},{9,10},{10,11},{11... | collective-permute-start | bytes 589832 | tf_op jit(solution)/shard_map/ppermute | solution.py:344
  46.8 7.0 %collective-permute-start.1 = (f32[384,128]{1,0:T(8,128)S(1)}, f32[384,128]{1,0:T(8,128)S(1)}, u32[]{:S(2)}, u32[]{:S(2)}) collective-permute-start(f32[384,128]{1,0:T(8,128)S(1)} %get-tuple-element.13), channel_id=1, source_target_pairs={{1,0},{2,1},{3,2},{4,3},{5,4},{6,5},{7,6},{9,8},{10,9},{11,10},{12... | collective-permute-start | bytes 589832 | tf_op jit(solution)/shard_map/ppermute | solution.py:345

commit v2 on v1

--- a/solution.py
+++ b/solution.py
@@ -89,12 +89,19 @@
     )
 
 
-def edges_kernel(recv_ref, low_ref, high_ref):
+def odd_row():
+    return lax.axis_index("az") & 1
+
+
+def edges_kernel(recv_ref, chip_ref, core_ref):
     lane = lanes_of((ACQ, 128))
+    odd = odd_row() == 1
     for part in range(2):
         rows = [acq_rows(recv_ref, part, r) for r in (0, 1, 3, 4)]
-        low_ref[part * ACQ : (part + 1) * ACQ, :] = jnp.where(lane < 64, rows[0], pltpu.roll(rows[1], 64, 1))
-        high_ref[part * ACQ : (part + 1) * ACQ, :] = jnp.where(lane < 64, pltpu.roll(rows[2], 64, 1), rows[3])
+        low = jnp.where(lane < 64, rows[0], pltpu.roll(rows[1], 64, 1))
+        high = jnp.where(lane < 64, pltpu.roll(rows[2], 64, 1), rows[3])
+        chip_ref[part * ACQ : (part + 1) * ACQ, :] = jnp.where(odd, high, low)
+        core_ref[part * ACQ : (part + 1) * ACQ, :] = jnp.where(odd, low, high)
 
 
 def pieces_of(x, count):
@@ -216,12 +223,14 @@
     lax.fori_loop(0, PAIRS // 16, some, 0, unroll=True)
 
 
-def pair_kernel(up_ref, down_ref, sums_ref, power_ref, pick_a, pick_b, out_ref, table, picked, terms, total, ends):
+def pair_kernel(chip_ref, core_ref, sums_ref, power_ref, pick_a, pick_b, out_ref, table, picked, terms, total, ends):
     fill(table)
     box = along_range()
     squares = []
-    for t, ref in enumerate((up_ref, down_ref)):
-        parts = [ref[part * ACQ : (part + 1) * ACQ, :] for part in range(2)]
+    odd = odd_row() == 1
+    for t, (even_ref, odd_ref) in enumerate(((chip_ref, core_ref), (core_ref, chip_ref))):
+        at = [slice(part * ACQ, (part + 1) * ACQ) for part in range(2)]
+        parts = [jnp.where(odd, odd_ref[rows, :], even_ref[rows, :]) for rows in at]
         for part, x in enumerate(parts):
             enter(table, x, t * 256 + part * 128)
         squares.append(parts[0] * parts[0] + parts[1] * parts[1])
@@ -339,13 +348,15 @@
     send = send.reshape(DEVS, CHUNK // 4, 4, 128)
     recv = lax.all_to_all(send, "acq", split_axis=0, concat_axis=0, tiled=True)
     recv = recv.reshape(DEVS * CHUNK, 128)
-    low, high = call(edges_kernel, (f32(2 * ACQ, 128), f32(2 * ACQ, 128)), [VMEM])(recv)
-    ends = lax.axis_size("az") - 1
-    up = lax.ppermute(high, "az", [(i, i + 1) for i in range(ends)])
-    down = lax.ppermute(low, "az", [(i + 1, i) for i in range(ends)])
+    chip, core = call(edges_kernel, (f32(2 * ACQ, 128), f32(2 * ACQ, 128)), [VMEM])(recv)
+    count = lax.axis_size("az")
+    across = [(i, i + 1) for i in range(1, count - 1, 2)]
+    inside = [(i, i + 1) for i in range(0, count, 2)]
+    chip = lax.ppermute(chip, "az", across + [(j, i) for i, j in across])
+    core = lax.ppermute(core, "az", inside + [(j, i) for i, j in inside])
     cost = pl.CostEstimate(flops=5 * 10**9, bytes_accessed=10**7, transcendentals=0)
     partial = call(own_kernel, OWN_OUTS, [VMEM], OWN_SCRATCH, cost_estimate=cost)(recv)
-    result = call(pair_kernel, f32(2 * DEVS, 128), [VMEM] * 6, PAIR_SCRATCH)(up, down, *partial)
+    result = call(pair_kernel, f32(2 * DEVS, 128), [VMEM] * 6, PAIR_SCRATCH)(chip, core, *partial)
     got = lax.all_to_all(result.reshape(DEVS, 2, 128), "acq", split_axis=0, concat_axis=0, tiled=True)
     outs = call(finish_kernel, (f32(32, 64),) * 3, [VMEM])(got.reshape(2 * DEVS, 128))
     return tuple(x.reshape(PAIR_DEV, 2, 64) for x in outs)

time: 71.5 us -> 68.4 us (0.957)
  starting transfers between devices: 7.99 us -> 6.16 us
  waiting for transfers between devices: 2.89 us -> 1.07 us
    ppermute x2, starting transfers between devices: 7.99 us -> 6.16 us  [the longest x1 6.07 us: per_device(): chip = lax.ppermute(chip, 'az', across + [(j, i) for i, j in across])]
    ppermute x2, waiting for transfers between devices: 2.89 us -> 1.07 us  [the longest x1 1.07 us: per_device(): chip = lax.ppermute(chip, 'az', across + [(j, i) for i, j in across])]
where the time goes in v2:
time: 68.4 us; the launch traced here: 67.9 us
  blocking collectives  50.7 us (74%)
  Pallas kernels  9.32 us (14%)
  starting transfers between devices  6.16 us (9%)
  waiting for transfers between devices  1.07 us (2%)
    all_to_all x1, blocking collectives, per_device(): recv = lax.all_to_all(send, 'acq', split_axis=0, concat_axis=0, tiled=True)  36.9 us
    all_to_all x1, blocking collectives, per_device(): lax.all_to_all(result.reshape(DEVS, 2, 128), 'acq', split_axis=0, concat_...  13.8 us
    ppermute x1, starting transfers between devices, per_device(): chip = lax.ppermute(chip, 'az', across + [(j, i) for i, j in across])  6.07 us
    pallas_call x1, Pallas kernels, per_device(): call(pair_kernel, f32(2 * DEVS, 128), [VMEM] * 6, PAIR_SCRATCH)  3.18 us
    pallas_call x1, Pallas kernels, per_device(): call(pack_kernel, f32(DEVS * CHUNK, 128), [HBM] * 3, (((ROWS, ACQ_DEV, RG...  3.11 us
    pallas_call x1, Pallas kernels, per_device(): call(own_kernel, OWN_OUTS, [VMEM], OWN_SCRATCH, cost_estimate=cost)(recv)  2.16 us
  transfers between devices with their start and end apart: 2, of which 1 were waited for; matrix products, arithmetic and copies ran while one was open for 0% of the time, Pallas kernels for 3%

profile of v2, /device:TPU:1, one launch (start us, length us, event | category | flops | bytes accessed | tf_op | source)
XLA Modules:
  0.0 67.9 jit_solution(11957342616578540527)
XLA Ops:
  0.6 3.1 %shard_map.58 = f32[1920,128]{1,0:T(8,128)} custom-call(f32[10,6,1280]{2,1,0:T(8,128)} %bitcast.15, f32[10,6,1280]{2,1,0:T(8,128)} %bitcast.16, s32[2,16]{1,0:T(2,128)} %bitcast.17), custom_call_target="tpu_custom_call" | custom-call | tf_op jit(solution)/shard_map/pallas_call | solution.py:336
  3.8 36.9 %all_to_all.10 = f32[32,15,4,128]{3,2,1,0:T(4,128)S(1)} all-to-all(f32[32,15,4,128]{3,2,1,0:T(4,128)} %bitcast.14), channel_id=1, replica_groups=mesh['acq'=32,'az'=8] {'acq'}, dimensions={0} | all-to-all | bytes 1966080 | tf_op jit(solution)/shard_map/all_to_all | solution.py:349
  40.6 0.2 shard_map.59
  40.8 6.1 %collective-permute-start = (f32[384,128]{1,0:T(8,128)S(1)}, f32[384,128]{1,0:T(8,128)S(1)}, u32[]{:S(2)}, u32[]{:S(2)}) collective-permute-start(f32[384,128]{1,0:T(8,128)S(1)} %get-tuple-element.12), channel_id=1, source_target_pairs={{1,2},{3,4},{5,6},{2,1},{4,3},{6,5},{9,10},{11,12},{13,14},{10,9},... | collective-permute-start | bytes 589832 | tf_op jit(solution)/shard_map/ppermute | solution.py:355
  46.9 0.1 collective-permute-start.1
  47.0 2.2 %shard_map.60 = (f32[1024,640]{1,0:T(8,128)S(1)}, f32[192,640]{1,0:T(8,128)S(1)}, bf16[512,256]{1,0:T(8,128)(2,1)S(1)}, bf16[512,768]{1,0:T(8,128)(2,1)S(1)}) custom-call(f32[1920,128]{1,0:T(8,128)S(1)} %bitcast.11), custom_call_target="tpu_custom_call" | custom-call | flops 5000000000 | bytes 10000000 | tf_op jit(solution)/shard_map/pallas_call | solution.py:358
  49.1 1.1 %collective-permute-done.chip_ref = f32[384,128]{1,0:T(8,128)S(1)} collective-permute-done((f32[384,128]{1,0:T(8,128)S(1)}, f32[384,128]{1,0:T(8,128)S(1)}, u32[]{:S(2)}, u32[]{:S(2)}) %collective-permute-start) | collective-permute-done | bytes 196640 | tf_op jit(solution)/shard_map/ppermute | solution.py:355
  50.2 0.0 collective-permute-done.1.core_ref
  50.2 3.2 %shard_map.61 = f32[64,128]{1,0:T(8,128)S(1)} custom-call(f32[384,128]{1,0:T(8,128)S(1)} %collective-permute-done.chip_ref, f32[384,128]{1,0:T(8,128)S(1)} %collective-permute-done.1.core_ref, f32[1024,640]{1,0:T(8,128)S(1)} %get-tuple-element.14.sums_ref, f32[192,640]{1,0:T(8,128)S(1)} %get-tuple-element.15.power_ref, ...), custom_call_target="tpu_custom_call" | custom-call | tf_op jit(solution)/shard_map/pallas_call | solution.py:359
  53.4 13.8 %all_to_all.11 = f32[32,2,128]{2,1,0:T(2,128)S(1)} all-to-all(f32[32,2,128]{2,1,0:T(2,128)S(1)} %bitcast.12), channel_id=1, replica_groups=mesh['acq'=32,'az'=8] {'acq'}, dimensions={0} | all-to-all | bytes 65536 | tf_op jit(solution)/shard_map/all_to_all | solution.py:360
  67.2 0.7 %shard_map.62 = (f32[32,64]{1,0:T(8,128)}, f32[32,64]{1,0:T(8,128)}, f32[32,64]{1,0:T(8,128)}) custom-call(f32[64,128]{1,0:T(8,128)S(1)} %bitcast.13), custom_call_target="tpu_custom_call" | custom-call | tf_op jit(solution)/shard_map/pallas_call | solution.py:361
Async XLA Ops:
  40.8 9.4 %collective-permute-start = (f32[384,128]{1,0:T(8,128)S(1)}, f32[384,128]{1,0:T(8,128)S(1)}, u32[]{:S(2)}, u32[]{:S(2)}) collective-permute-start(f32[384,128]{1,0:T(8,128)S(1)} %get-tuple-element.12), channel_id=1, source_target_pairs={{1,2},{3,4},{5,6},{2,1},{4,3},{6,5},{9,10},{11,12},{13,14},{10,9},... | collective-permute-start | bytes 589832 | tf_op jit(solution)/shard_map/ppermute | solution.py:355
  46.9 3.3 %collective-permute-start.1 = (f32[384,128]{1,0:T(8,128)S(1)}, f32[384,128]{1,0:T(8,128)S(1)}, u32[]{:S(2)}, u32[]{:S(2)}) collective-permute-start(f32[384,128]{1,0:T(8,128)S(1)} %get-tuple-element.13), channel_id=1, source_target_pairs={{0,1},{2,3},{4,5},{6,7},{1,0},{3,2},{5,4},{7,6},{8,9},{10,11},{12,... | collective-permute-start | bytes 589832 | tf_op jit(solution)/shard_map/ppermute | solution.py:356

commit v3 on v2

v3 whole, which is shorter than its diff:
```python
import jax
import jax.numpy as jnp
from jax import lax
from jax.experimental import pallas as pl
from jax.experimental.pallas import tpu as pltpu
from jax.sharding import PartitionSpec as P

DEVS = 32
ACQ_DEV = 6
ACQ = DEVS * ACQ_DEV
PAIR_DEV = 16
PAIRS = DEVS * PAIR_DEV
ROWS = 10
HALF = 5
RG = 1280
STEP = 40
WIDE = STEP + 19
CHUNK = 60
K = 256
F32 = jnp.float32
BF16 = jnp.bfloat16
VMEM = pl.BlockSpec(memory_space=pltpu.VMEM)
HBM = pl.BlockSpec(memory_space=pltpu.HBM)
BIG = 3.38e38
PART = 8 * ACQ_DEV


def lanes_of(shape):
    return lax.broadcasted_iota(jnp.int32, shape, len(shape) - 1)


def odd_row():
    return lax.axis_index("az") & 1


def pack_kernel(re_hbm, im_hbm, pairs_hbm, out_hbm, re_ref, im_ref, pairs_ref, later, chunks, sems):
    odd = odd_row()
    copies = [
        pltpu.make_async_copy(source, target, sems.at[n])
        for n, (source, target) in enumerate(((pairs_hbm, pairs_ref), (re_hbm, re_ref), (im_hbm, im_ref)))
    ]
    for copy in copies:
        copy.start()
    lane = lanes_of((ACQ_DEV, 128))
    wide = lanes_of((PAIR_DEV, 128))
    copies[0].wait()
    acq = pairs_ref[...]
    group = (acq * 171) >> 10
    local = (acq - ACQ_DEV * group) * 8 + (group & 7)
    order = lax.broadcasted_iota(jnp.int32, (2, PAIR_DEV), 0)
    index = (local + jnp.where(order == 0, 0, (group >> 3) * PART)).astype(F32)
    square = (PAIR_DEV, PAIR_DEV)
    diagonal = lax.broadcasted_iota(jnp.int32, square, 0) == lax.broadcasted_iota(jnp.int32, square, 1)
    columns = [
        jnp.sum(jnp.where(diagonal, jnp.broadcast_to(index[w : w + 1, :], square), 0.0), axis=1, keepdims=True)
        for w in range(2)
    ]
    first, second = [jnp.broadcast_to(column, (PAIR_DEV, 128)) for column in columns]
    tiles = RG // 128
    for part, ref in enumerate((re_ref, im_ref)):
        copies[1 + part].wait()
        for r in range(HALF):
            row = r + HALF + odd * (9 - 2 * (r + HALF))
            for t in range(tiles):
                x = ref[row, :, t * 128 : (t + 1) * 128]
                later[part * HALF + r, :, t * 128 : (t + 1) * 128] = pltpu.roll(x, 64, 1)
    out_copies = []
    for d in range(DEVS):
        start = STEP * d - 10
        k = start // 128
        off = start - 128 * k
        spans = []
        for t, low, high in ((k, off, min(128, off + WIDE)), (k + 1, 0, off + WIDE - 128)):
            if low < high and 0 <= t < tiles:
                spans.append((t, False, low, high))
                shifted = [(low + 64, min(high + 64, 128)), (max(low + 64, 128) - 128, high + 64 - 128)]
                spans += [(t, True, x, y) for x, y in shifted if x < y]
        masks = [(lane >= low) & (lane < high) for _, _, low, high in spans]
        for part, ref in enumerate((re_ref, im_ref)):
            for r in range(HALF):
                row = r + odd * (9 - 2 * r)
                mixed = jnp.zeros((ACQ_DEV, 128), F32)
                for (t, shifted, _, _), mask in zip(spans, masks):
                    at = slice(t * 128, (t + 1) * 128)
                    mixed = jnp.where(mask, later[part * HALF + r, :, at] if shifted else ref[row, :, at], mixed)
                top = d * CHUNK + (part * HALF + r) * ACQ_DEV
                chunks[top : top + ACQ_DEV, :] = pltpu.roll(mixed, 128 - off, 1) if off else mixed
        head = chunks[d * CHUNK : d * CHUNK + PAIR_DEV, :]
        head = jnp.where(wide == 60, first, jnp.where(wide == 61, second, head))
        chunks[d * CHUNK : d * CHUNK + PAIR_DEV, :] = head
        if d % 8 == 7:
            rows = pl.ds((d - 7) * CHUNK, 8 * CHUNK)
            out_copies.append(pltpu.make_async_copy(chunks.at[rows, :], out_hbm.at[rows, :], sems.at[3 + d // 8]))
            out_copies[-1].start()
    for copy in out_copies:
        copy.wait()


def acq_rows(recv_ref, part, r):
    base = (part * HALF + r) * ACQ_DEV
    return jnp.concatenate(
        [recv_ref[pl.ds(base + a + 8 * g * CHUNK, 8, stride=CHUNK), :] for g in range(4) for a in range(ACQ_DEV)],
        axis=0,
    )


def edges_kernel(recv_ref, chip_ref, core_ref):
    lane = lanes_of((ACQ, 128))
    for part in range(2):
        v0, v1, v3, v4 = [acq_rows(recv_ref, part, r) for r in (0, 1, 3, 4)]
        rows = slice(part * ACQ, (part + 1) * ACQ)
        chip_ref[rows, :] = jnp.where(lane < 64, v0, pltpu.roll(v1, 64, 1))
        core_ref[rows, :] = jnp.where(lane < 64, pltpu.roll(v3, 64, 1), v4)
    chip_ref[2 * ACQ :, :] = jnp.zeros((8, 128), F32)


def pieces_of(x, count):
    out = []
    for n in range(count):
        piece = x.astype(BF16)
        out.append(piece)
        if n + 1 < count:
            x = x - piece.astype(F32)
    return out


def clamp(x):
    return jnp.minimum(jnp.maximum(x, -BIG), BIG)


def dot(x, y):
    return jnp.dot(x, y, preferred_element_type=F32)


def fill(table):
    for p in range(3):
        table[p * K + ACQ : (p + 1) * K, :] = jnp.zeros((K - ACQ, table.shape[1]), BF16)


def enter(table, x, at):
    for p, piece in enumerate(pieces_of(clamp(x), 3)):
        table[p * K : p * K + ACQ, at : at + x.shape[1]] = piece


def along_range():
    shape = (128, 128)
    k = lax.broadcasted_iota(jnp.int32, shape, 0)
    n = lax.broadcasted_iota(jnp.int32, shape, 1)
    c = n & 63
    first = jnp.where(c < STEP, c, jnp.where(c < STEP + 4, 10 + 20 * (c & 1), -1000))
    sample = k & 63
    inside = ((k >> 6) == (n >> 6)) & (sample >= first) & (sample <= first + 19)
    box = jnp.where(inside, 1.0, 0.0).astype(BF16)
    return jnp.concatenate([box, box], axis=0)


def choose(pick_a, pick_b, table, picked, at, width):
    columns = slice(at, at + width)
    picked[PAIRS:, columns] = dot(pick_b[...], table[:, columns])
    for g in range(4):
        few = jnp.concatenate([table[p * K + g * PART : p * K + (g + 1) * PART, columns] for p in range(3)], axis=0)
        picked[128 * g : 128 * (g + 1), columns] = dot(pick_a[128 * g : 128 * (g + 1), : 3 * PART], few)


def cross(picked, top, count):
    fields = [[], []]
    for t in range(count):
        ra = picked[pl.ds(top, 16), t * 256 : t * 256 + 128]
        ia = picked[pl.ds(top, 16), t * 256 + 128 : t * 256 + 256]
        rb = picked[pl.ds(top + PAIRS, 16), t * 256 : t * 256 + 128]
        ib = picked[pl.ds(top + PAIRS, 16), t * 256 + 128 : t * 256 + 256]
        fields[0].append(ra * rb + ia * ib)
        fields[1].append(ia * rb - ra * ib)
    return fields


def own_rows(v):
    v0, v1, v2, v3, v4 = v
    low = lanes_of(v0.shape) < 64
    next_one = pltpu.roll(jnp.where(low, v4, v0), 64, 1)
    next_two = next_one + pltpu.roll(jnp.where(low, v3, v1), 64, 1)
    v12, v34 = v1 + v2, v3 + v4
    v012, v234 = v0 + v12, v2 + v34
    return [
        v012 + jnp.where(low, 0.0, next_two),
        (v012 + v3) + jnp.where(low, 0.0, next_one),
        v012 + v34,
        (v1 + v234) + jnp.where(low, next_one, 0.0),
        v234 + jnp.where(low, next_two, 0.0),
    ]


def edge_rows(near, far, edge, low):
    inside = (lanes_of(edge.shape) < 64) == low
    return near + jnp.where(inside, edge + pltpu.roll(edge, 64, 1), 0.0), far + jnp.where(inside, edge, 0.0)


def store_terms(terms, top, x):
    for n, piece in enumerate(pieces_of(x, 2)):
        terms[pl.ds(top, 16), n * 128 : (n + 1) * 128] = piece


def enter_power(table, x, box, at):
    enter(table, dot(jnp.concatenate(pieces_of(x, 2), axis=1), box), at)


def coherence_of(total, picked, top, row, at):
    x0 = total[pl.ds(top + 2 * row * PAIRS, 16), :]
    x1 = total[pl.ds(top + (2 * row + 1) * PAIRS, 16), :]
    wa = picked[pl.ds(top, 16), at : at + 128]
    wb = picked[pl.ds(top + PAIRS, 16), at : at + 128]
    inverse = lax.rsqrt(wa * wb + 1e-06)
    num = x0 * x0 + x1 * x1
    return num * lax.rsqrt(jnp.maximum(num, 1e-37)) * inverse, x0, x1, inverse


def for_pairs(body):
    def step(g, carry):
        body(pl.multiple_of(16 * g, 16))
        return carry

    lax.fori_loop(0, PAIRS // 16, step, 0, unroll=True)


def own_kernel(
    recv_ref, up_ref, down_ref, up_power, down_power, pick_a, pick_b, value_ref, table, picked, terms, total
):
    lane = lanes_of((128, K))
    few = lane - PART * ((lane * 342) >> 14)
    for g in range(4):
        head = jnp.concatenate([recv_ref[pl.ds(8 * g * CHUNK + p, 8, stride=CHUNK), :] for p in range(PAIR_DEV)], axis=0)
        rows = slice(128 * g, 128 * (g + 1))
        index = jnp.broadcast_to(head[:, 60:61], (128, K))
        pick_a[rows, :] = jnp.where(index == few.astype(F32), 1.0, 0.0).astype(BF16)
        index = jnp.broadcast_to(head[:, 61:62], (128, K))
        hot = jnp.where(index == lane.astype(F32), 1.0, 0.0).astype(BF16)
        for p in range(3):
            pick_b[rows, p * K : (p + 1) * K] = hot
    fill(table)
    box = along_range()
    squares = []
    for t in range(HALF):
        parts = [acq_rows(recv_ref, part, t) for part in range(2)]
        for part, x in enumerate(parts):
            enter(table, x, t * 256 + part * 128)
        squares.append(parts[0] * parts[0] + parts[1] * parts[1])
        choose(pick_a, pick_b, table, picked, t * 256, 256)
    sums = own_rows(squares)
    up_power[:, 0:128], up_power[:, 128:256] = sums[0], sums[1]
    down_power[:, 0:128], down_power[:, 128:256] = sums[4], sums[3]
    enter_power(table, sums[2], box, HALF * 256)
    choose(pick_a, pick_b, table, picked, HALF * 256, 128)

    def rows(top):
        for f, field in enumerate(cross(picked, top, HALF)):
            x = own_rows(field)
            here = pl.ds(top + f * PAIRS, 16)
            up_ref[here, 0:128], up_ref[here, 128:256] = x[0], x[1]
            down_ref[here, 0:128], down_ref[here, 128:256] = x[4], x[3]
            store_terms(terms, top + f * PAIRS, x[2])

    for_pairs(rows)
    total[...] = dot(terms[...], box)
    lane16 = lanes_of((16, 128)) & 63

    def some(top):
        size, x0, x1, inverse = coherence_of(total, picked, top, 0, HALF * 256)
        value_ref[pl.ds(top, 16), :] = jnp.where(lane16 < STEP, size, jnp.where(lane16 < STEP + 2, x0, x1) * inverse)

    for_pairs(some)


def edge_coherence(edge_ref, sums_ref, power_ref, pick_a, pick_b, table, picked, terms, total, low):
    fill(table)
    box = along_range()
    parts = [edge_ref[part * ACQ : (part + 1) * ACQ, :] for part in range(2)]
    for part, x in enumerate(parts):
        enter(table, x, part * 128)
    choose(pick_a, pick_b, table, picked, 0, 256)
    square = parts[0] * parts[0] + parts[1] * parts[1]
    for n, x in enumerate(edge_rows(power_ref[:, 0:128], power_ref[:, 128:256], square, low)):
        enter_power(table, x, box, 256 + n * 128)
    choose(pick_a, pick_b, table, picked, 256, 256)

    def rows(top):
        for f, field in enumerate(cross(picked, top, 1)):
            here = pl.ds(top + f * PAIRS, 16)
            for n, x in enumerate(edge_rows(sums_ref[here, 0:128], sums_ref[here, 128:256], field[0], low)):
                store_terms(terms, top + (2 * n + f) * PAIRS, x)

    for_pairs(rows)
    total[...] = dot(terms[...], box)


def edge_value(value_ref, total, picked, top):
    size = coherence_of(total, picked, top, 0, 256)[0] + coherence_of(total, picked, top, 1, 384)[0]
    return value_ref[pl.ds(top, 16), :] + jnp.where((lanes_of(size.shape) & 63) < STEP, size, 0.0)


def core_kernel(core_ref, sums_ref, power_ref, pick_a, pick_b, value_ref, out_ref, table, picked, terms, total):
    edge_coherence(core_ref, sums_ref, power_ref, pick_a, pick_b, table, picked, terms, total, False)

    def some(top):
        out_ref[pl.ds(top, 16), :] = edge_value(value_ref, total, picked, top)

    for_pairs(some)


def chip_kernel(chip_ref, sums_ref, power_ref, pick_a, pick_b, value_ref, out_ref, table, picked, terms, total, ends):
    edge_coherence(chip_ref, sums_ref, power_ref, pick_a, pick_b, table, picked, terms, total, True)

    def some(top):
        for p, piece in enumerate(pieces_of(edge_value(value_ref, total, picked, top), 3)):
            ends[pl.ds(top, 16), p * 128 : (p + 1) * 128] = piece

    for_pairs(some)

    n = lax.broadcasted_iota(jnp.int32, (128, 256), 0)
    m = lax.broadcasted_iota(jnp.int32, (128, 256), 1)
    c, j, o = n & 63, m >> 7, (m >> 5) & 3
    first = jnp.where(o == 0, 20 * j, jnp.where(o == 3, 1000, STEP - 2 + 2 * o + j))
    last = first + jnp.where(o == 0, 19, 0)
    same = ((n >> 6) == ((m & 1) ^ odd_row())) & (c >= first) & (c <= last)
    spread = jnp.where(same, 1.0, 0.0).astype(BF16)
    result = dot(ends[...], jnp.concatenate([spread] * 3, axis=0))
    owner = (lanes_of((8, 128)) >> 1) & 15
    for j in range(2):
        for g in range(4):
            out = None
            for p in range(PAIR_DEV):
                top = 128 * g + 8 * p
                rows_p = result[top : top + 8, j * 128 : (j + 1) * 128]
                out = rows_p if out is None else jnp.where(owner == p, rows_p, out)
            out_ref[pl.ds(16 * g + j, 8, stride=2), :] = out


def finish_kernel(got_ref, coh_ref, re_ref, im_ref):
    turned = jnp.transpose(got_ref[...])
    coh_ref[...] = turned[0:32] * 0.01
    re_ref[...] = turned[32:64]
    im_ref[...] = turned[64:96]


def call(kernel, outs, specs, scratch=(), limit=40, out_spec=VMEM, **more):
    return pl.pallas_call(
        kernel,
        out_shape=outs,
        in_specs=specs,
        out_specs=jax.tree.map(lambda _: out_spec, outs),
        scratch_shapes=[pltpu.VMEM(*x) if isinstance(x, tuple) else x for x in scratch],
        compiler_params=pltpu.CompilerParams(vmem_limit_bytes=limit * 1024 * 1024),
        **more,
    )


def f32(*shape):
    return jax.ShapeDtypeStruct(shape, F32)


def bf16(*shape):
    return jax.ShapeDtypeStruct(shape, BF16)


EDGE_OUTS = (f32(2 * PAIRS, 256),) * 2 + (f32(ACQ, 256),) * 2
OWN_OUTS = EDGE_OUTS + (bf16(PAIRS, K), bf16(PAIRS, 3 * K), f32(PAIRS, 128))
OWN_SCRATCH = (
    ((3 * K, HALF * 256 + 128), BF16),
    ((2 * PAIRS, HALF * 256 + 128), F32),
    ((2 * PAIRS, 256), BF16),
    ((2 * PAIRS, 128), F32),
)
EDGE_SCRATCH = (
    ((3 * K, 512), BF16),
    ((2 * PAIRS, 512), F32),
    ((4 * PAIRS, 256), BF16),
    ((4 * PAIRS, 128), F32),
)
CHIP_SCRATCH = EDGE_SCRATCH + (((PAIRS, 3 * 128), BF16),)


def per_device(slc_re, slc_im, pairs):
    send = call(
        pack_kernel,
        f32(DEVS * CHUNK, 128),
        [HBM] * 3,
        (
            ((ROWS, ACQ_DEV, RG), F32),
            ((ROWS, ACQ_DEV, RG), F32),
            ((2, PAIR_DEV), jnp.int32),
            ((2 * HALF, ACQ_DEV, RG), F32),
            ((DEVS * CHUNK, 128), F32),
            pltpu.SemaphoreType.DMA((7,)),
        ),
        limit=60,
        out_spec=HBM,
    )(jnp.transpose(slc_re, (1, 0, 2)), jnp.transpose(slc_im, (1, 0, 2)), pairs.T)
    send = send.reshape(DEVS, CHUNK // 4, 4, 128)
    recv = lax.all_to_all(send, "acq", split_axis=0, concat_axis=0, tiled=True)
    recv = recv.reshape(DEVS * CHUNK, 128)
    chip, core = call(edges_kernel, (f32(2 * ACQ + 8, 128), f32(2 * ACQ, 128)), [VMEM])(recv)
    count = lax.axis_size("az")
    across = [(i, i + 1) for i in range(1, count - 1, 2)]
    inside = [(i, i + 1) for i in range(0, count, 2)]
    chip = lax.ppermute(chip, "az", across + [(j, i) for i, j in across])
    core = lax.ppermute(core, "az", inside + [(j, i) for i, j in inside])
    cost = [pl.CostEstimate(flops=n, bytes_accessed=n, transcendentals=0) for n in (10**3, 10**3)]
    own = call(own_kernel, OWN_OUTS, [VMEM], OWN_SCRATCH, cost_estimate=cost[0])(recv)
    up, down, up_power, down_power, pick_a, pick_b, value = own
    value = call(core_kernel, f32(PAIRS, 128), [VMEM] * 6, EDGE_SCRATCH, cost_estimate=cost[1])(
        core, down, down_power, pick_a, pick_b, value
    )
    result = call(chip_kernel, f32(2 * DEVS, 128), [VMEM] * 6, CHIP_SCRATCH)(
        chip, up, up_power, pick_a, pick_b, value
    )
    got = lax.all_to_all(result.reshape(DEVS, 2, 128), "acq", split_axis=0, concat_axis=0, tiled=True)
    outs = call(finish_kernel, (f32(32, 64),) * 3, [VMEM])(got.reshape(2 * DEVS, 128))
    return tuple(x.reshape(PAIR_DEV, 2, 64) for x in outs)


def solution(mesh):
    in_specs = (P("acq", "az", None), P("acq", "az", None), P("acq", None))
    out_specs = (P("acq", "az", None), P("acq", "az", None), P("acq", "az", None))
    return jax.shard_map(per_device, mesh=mesh, in_specs=in_specs, out_specs=out_specs, check_vma=False)
```

time: 68.4 us -> 66.6 us (0.974)
  waiting for transfers between devices: 1.07 us -> 0.01 us
    ppermute x1, waiting for transfers between devices: 1.07 us -> 0.01 us  [per_device(): chip = lax.ppermute(chip, 'az', across + [(j, i) for i, j in across])]
    pallas_call x3 -> x4, Pallas kernels: 5.51 us -> 5.6 us  [the longest x1 2.59 us: per_device(): call(own_kernel, OWN_OUTS, [VMEM], OWN_SCRATCH, cost_estimate=cost[0])(recv)]
  transfers between devices with their start and end apart: 2 -> 2, of which waited for: 1 -> 0; matrix products, arithmetic and copies ran while one was open for 0% -> 0% of each run, Pallas kernels for 3% -> 6%
where the time goes in v3:
time: 66.6 us; the launch traced here: 66 us
  blocking collectives  50.4 us (76%)
  Pallas kernels  8.76 us (13%)
  starting transfers between devices  6.16 us (9%)
  between operations  0.69 us (1%)
    all_to_all x1, blocking collectives, per_device(): recv = lax.all_to_all(send, 'acq', split_axis=0, concat_axis=0, tiled=True)  36.9 us
    all_to_all x1, blocking collectives, per_device(): lax.all_to_all(result.reshape(DEVS, 2, 128), 'acq', split_axis=0, concat_...  13.5 us
    ppermute x1, starting transfers between devices, per_device(): chip = lax.ppermute(chip, 'az', across + [(j, i) for i, j in across])  6.07 us
    pallas_call x1, Pallas kernels, per_device(): call(own_kernel, OWN_OUTS, [VMEM], OWN_SCRATCH, cost_estimate=cost[0])(recv)  2.59 us
    pallas_call x1, Pallas kernels, per_device(): call(pack_kernel, f32(DEVS * CHUNK, 128), [HBM] * 3, (((ROWS, ACQ_DEV, RG...  2.47 us
    pallas_call x1, Pallas kernels, per_device(): call(chip_kernel, f32(2 * DEVS, 128), [VMEM] * 6, CHIP_SCRATCH)  1.63 us
  transfers between devices with their start and end apart: 2, of which 0 were waited for; matrix products, arithmetic and copies ran while one was open for 0% of the time, Pallas kernels for 6%

profile of v3, /device:TPU:1, one launch (start us, length us, event | category | flops | bytes accessed | tf_op | source)
XLA Modules:
  0.0 66.0 jit_solution(833780048334139683)
XLA Ops:
  0.6 2.5 %shard_map.58 = f32[1920,128]{1,0:T(8,128)} custom-call(f32[10,6,1280]{2,1,0:T(8,128)} %bitcast.15, f32[10,6,1280]{2,1,0:T(8,128)} %bitcast.16, s32[2,16]{1,0:T(2,128)} %bitcast.17), custom_call_target="tpu_custom_call" | custom-call | tf_op jit(solution)/shard_map/pallas_call | solution.py:382
  3.1 36.9 %all_to_all.10 = f32[32,15,4,128]{3,2,1,0:T(4,128)S(1)} all-to-all(f32[32,15,4,128]{3,2,1,0:T(4,128)} %bitcast.14), channel_id=1, replica_groups=mesh['acq'=32,'az'=8] {'acq'}, dimensions={0} | all-to-all | bytes 1966080 | tf_op jit(solution)/shard_map/all_to_all | solution.py:398
  40.0 0.2 shard_map.59
  40.1 6.1 %collective-permute-start = (f32[392,128]{1,0:T(8,128)S(1)}, f32[392,128]{1,0:T(8,128)S(1)}, u32[]{:S(2)}, u32[]{:S(2)}) collective-permute-start(f32[392,128]{1,0:T(8,128)S(1)} %get-tuple-element.15), channel_id=1, source_target_pairs={{1,2},{3,4},{5,6},{2,1},{4,3},{6,5},{9,10},{11,12},{13,14},{10,9},... | collective-permute-start | bytes 602120 | tf_op jit(solution)/shard_map/ppermute | solution.py:404
  46.2 0.1 collective-permute-start.1
  46.3 2.6 %shard_map.60 = (f32[1024,256]{1,0:T(8,128)S(1)}, f32[1024,256]{1,0:T(8,128)S(1)}, f32[192,256]{1,0:T(8,128)S(1)}, f32[192,256]{1,0:T(8,128)S(1)}, bf16[512,256]...) custom-call(f32[1920,128]{1,0:T(8,128)S(1)} %bitcast.11), custom_call_target="tpu_custom_call" | custom-call | flops 1000 | bytes 1000 | tf_op jit(solution)/shard_map/pallas_call | solution.py:407
  48.9 0.0 collective-permute-done.1.core_ref
  48.9 1.2 %shard_map.61.value_ref = f32[512,128]{1,0:T(8,128)S(1)} custom-call(f32[384,128]{1,0:T(8,128)S(1)} %collective-permute-done.1.core_ref, f32[1024,256]{1,0:T(8,128)S(1)} %get-tuple-element.21.sums_ref, f32[192,256]{1,0:T(8,128)S(1)} %get-tuple-element.22.power_ref, bf16[512,256]{1,0:T(8,128)(2,1)S(1)} %get-tuple-element.18.pick_a, ...), custom_call_target="tpu_custom_call" | custom-call | flops 1000 | bytes 1000 | tf_op jit(solution)/shard_map/pallas_call | solution.py:409
  50.1 0.0 collective-permute-done.chip_ref
  50.1 1.6 %shard_map.62 = f32[64,128]{1,0:T(8,128)S(1)} custom-call(f32[392,128]{1,0:T(8,128)S(1)} %collective-permute-done.chip_ref, f32[1024,256]{1,0:T(8,128)S(1)} %get-tuple-element.16.sums_ref, f32[192,256]{1,0:T(8,128)S(1)} %get-tuple-element.17.power_ref, bf16[512,256]{1,0:T(8,128)(2,1)S(1)} %get-tuple-element.18.pick_a, ...), custom_call_target="tpu_custom_call" | custom-call | tf_op jit(solution)/shard_map/pallas_call | solution.py:412
  51.8 13.5 %all_to_all.11 = f32[32,2,128]{2,1,0:T(2,128)S(1)} all-to-all(f32[32,2,128]{2,1,0:T(2,128)S(1)} %bitcast.12), channel_id=1, replica_groups=mesh['acq'=32,'az'=8] {'acq'}, dimensions={0} | all-to-all | bytes 65536 | tf_op jit(solution)/shard_map/all_to_all | solution.py:415
  65.3 0.7 %shard_map.63 = (f32[32,64]{1,0:T(8,128)}, f32[32,64]{1,0:T(8,128)}, f32[32,64]{1,0:T(8,128)}) custom-call(f32[64,128]{1,0:T(8,128)S(1)} %bitcast.13), custom_call_target="tpu_custom_call" | custom-call | tf_op jit(solution)/shard_map/pallas_call | solution.py:416
Async XLA Ops:
  40.1 10.0 %collective-permute-start = (f32[392,128]{1,0:T(8,128)S(1)}, f32[392,128]{1,0:T(8,128)S(1)}, u32[]{:S(2)}, u32[]{:S(2)}) collective-permute-start(f32[392,128]{1,0:T(8,128)S(1)} %get-tuple-element.15), channel_id=1, source_target_pairs={{1,2},{3,4},{5,6},{2,1},{4,3},{6,5},{9,10},{11,12},{13,14},{10,9},... | collective-permute-start | bytes 602120 | tf_op jit(solution)/shard_map/ppermute | solution.py:404
  46.2 2.7 %collective-permute-start.1 = (f32[384,128]{1,0:T(8,128)S(1)}, f32[384,128]{1,0:T(8,128)S(1)}, u32[]{:S(2)}, u32[]{:S(2)}) collective-permute-start(f32[384,128]{1,0:T(8,128)S(1)} %get-tuple-element.20), channel_id=1, source_target_pairs={{0,1},{2,3},{4,5},{6,7},{1,0},{3,2},{5,4},{7,6},{8,9},{10,11},{12,... | collective-permute-start | bytes 589832 | tf_op jit(solution)/shard_map/ppermute | solution.py:405

commit v4 on v3

--- a/solution.py
+++ b/solution.py
@@ -33,7 +33,7 @@
     return lax.axis_index("az") & 1
 
 
-def pack_kernel(re_hbm, im_hbm, pairs_hbm, out_hbm, re_ref, im_ref, pairs_ref, later, chunks, sems):
+def pack_kernel(re_hbm, im_hbm, pairs_hbm, chunks, re_ref, im_ref, pairs_ref, later, sems):
     odd = odd_row()
     copies = [
         pltpu.make_async_copy(source, target, sems.at[n])
@@ -64,7 +64,6 @@
             for t in range(tiles):
                 x = ref[row, :, t * 128 : (t + 1) * 128]
                 later[part * HALF + r, :, t * 128 : (t + 1) * 128] = pltpu.roll(x, 64, 1)
-    out_copies = []
     for d in range(DEVS):
         start = STEP * d - 10
         k = start // 128
@@ -88,12 +87,6 @@
         head = chunks[d * CHUNK : d * CHUNK + PAIR_DEV, :]
         head = jnp.where(wide == 60, first, jnp.where(wide == 61, second, head))
         chunks[d * CHUNK : d * CHUNK + PAIR_DEV, :] = head
-        if d % 8 == 7:
-            rows = pl.ds((d - 7) * CHUNK, 8 * CHUNK)
-            out_copies.append(pltpu.make_async_copy(chunks.at[rows, :], out_hbm.at[rows, :], sems.at[3 + d // 8]))
-            out_copies[-1].start()
-    for copy in out_copies:
-        copy.wait()
 
 
 def acq_rows(recv_ref, part, r):
@@ -388,12 +381,11 @@
             ((ROWS, ACQ_DEV, RG), F32),
             ((2, PAIR_DEV), jnp.int32),
             ((2 * HALF, ACQ_DEV, RG), F32),
-            ((DEVS * CHUNK, 128), F32),
-            pltpu.SemaphoreType.DMA((7,)),
+            pltpu.SemaphoreType.DMA((3,)),
         ),
-        limit=60,
-        out_spec=HBM,
-    )(jnp.transpose(slc_re, (1, 0, 2)), jnp.transpose(slc_im, (1, 0, 2)), pairs.T)
+        limit=40,
+        out_spec=VMEM,
+    )(*[pltpu.with_memory_space_constraint(x, pltpu.HBM) for x in (jnp.transpose(slc_re, (1, 0, 2)), jnp.transpose(slc_im, (1, 0, 2)), pairs.T)])
     send = send.reshape(DEVS, CHUNK // 4, 4, 128)
     recv = lax.all_to_all(send, "acq", split_axis=0, concat_axis=0, tiled=True)
     recv = recv.reshape(DEVS * CHUNK, 128)

time: 66.6 us -> 65.6 us (0.985)
  Pallas kernels: 8.76 us -> 8.03 us
    pallas_call x1, Pallas kernels: 2.47 us -> 1.74 us  [per_device(): call(pack_kernel, f32(DEVS * CHUNK, 128), [HBM] * 3, (((ROWS, ACQ_DEV, RG...]
where the time goes in v4:
time: 65.6 us; the launch traced here: 65.1 us
  blocking collectives  50.2 us (77%)
  Pallas kernels  8.03 us (12%)
  starting transfers between devices  6.18 us (9%)
  between operations  0.69 us (1%)
    all_to_all x1, blocking collectives, per_device(): recv = lax.all_to_all(send, 'acq', split_axis=0, concat_axis=0, tiled=True)  36.6 us
    all_to_all x1, blocking collectives, per_device(): lax.all_to_all(result.reshape(DEVS, 2, 128), 'acq', split_axis=0, concat_...  13.5 us
    ppermute x1, starting transfers between devices, per_device(): chip = lax.ppermute(chip, 'az', across + [(j, i) for i, j in across])  6.08 us
    pallas_call x1, Pallas kernels, per_device(): call(own_kernel, OWN_OUTS, [VMEM], OWN_SCRATCH, cost_estimate=cost[0])(recv)  2.59 us
    pallas_call x1, Pallas kernels, per_device(): call(pack_kernel, f32(DEVS * CHUNK, 128), [HBM] * 3, (((ROWS, ACQ_DEV, RG...  1.74 us
    pallas_call x1, Pallas kernels, per_device(): call(chip_kernel, f32(2 * DEVS, 128), [VMEM] * 6, CHIP_SCRATCH)  1.63 us
  transfers between devices with their start and end apart: 2, of which 0 were waited for; matrix products, arithmetic and copies ran while one was open for 0% of the time, Pallas kernels for 6%

profile of v4, /device:TPU:1, one launch (start us, length us, event | category | flops | bytes accessed | tf_op | source)
XLA Modules:
  0.0 65.1 jit_solution(14637754159686760062)
XLA Ops:
  0.6 1.7 %shard_map.58 = f32[1920,128]{1,0:T(8,128)S(1)} custom-call(f32[10,6,1280]{2,1,0:T(8,128)} %bitcast.15, f32[10,6,1280]{2,1,0:T(8,128)} %bitcast.16, s32[2,16]{1,0:T(2,128)} %bitcast.17), custom_call_target="tpu_custom_call" | custom-call | tf_op jit(solution)/shard_map/pallas_call | solution.py:375
  2.4 36.6 %all_to_all.10 = f32[32,15,4,128]{3,2,1,0:T(4,128)S(1)} all-to-all(f32[32,15,4,128]{3,2,1,0:T(4,128)S(1)} %bitcast.12), channel_id=1, replica_groups=mesh['acq'=32,'az'=8] {'acq'}, dimensions={0} | all-to-all | bytes 1966080 | tf_op jit(solution)/shard_map/all_to_all | solution.py:390
  39.0 0.2 shard_map.59
  39.2 6.1 %collective-permute-start = (f32[392,128]{1,0:T(8,128)S(1)}, f32[392,128]{1,0:T(8,128)S(1)}, u32[]{:S(2)}, u32[]{:S(2)}) collective-permute-start(f32[392,128]{1,0:T(8,128)S(1)} %get-tuple-element.15), channel_id=1, source_target_pairs={{1,2},{3,4},{5,6},{2,1},{4,3},{6,5},{9,10},{11,12},{13,14},{10,9},... | collective-permute-start | bytes 602120 | tf_op jit(solution)/shard_map/ppermute | solution.py:396
  45.3 0.1 collective-permute-start.1
  45.4 2.6 %shard_map.60 = (f32[1024,256]{1,0:T(8,128)S(1)}, f32[1024,256]{1,0:T(8,128)S(1)}, f32[192,256]{1,0:T(8,128)S(1)}, f32[192,256]{1,0:T(8,128)S(1)}, bf16[512,256]...) custom-call(f32[1920,128]{1,0:T(8,128)S(1)} %bitcast.11), custom_call_target="tpu_custom_call" | custom-call | flops 1000 | bytes 1000 | tf_op jit(solution)/shard_map/pallas_call | solution.py:399
  48.0 0.0 collective-permute-done.1.core_ref
  48.0 1.2 %shard_map.61.value_ref = f32[512,128]{1,0:T(8,128)S(1)} custom-call(f32[384,128]{1,0:T(8,128)S(1)} %collective-permute-done.1.core_ref, f32[1024,256]{1,0:T(8,128)S(1)} %get-tuple-element.21.sums_ref, f32[192,256]{1,0:T(8,128)S(1)} %get-tuple-element.22.power_ref, bf16[512,256]{1,0:T(8,128)(2,1)S(1)} %get-tuple-element.18.pick_a, ...), custom_call_target="tpu_custom_call" | custom-call | flops 1000 | bytes 1000 | tf_op jit(solution)/shard_map/pallas_call | solution.py:401
  49.2 0.0 collective-permute-done.chip_ref
  49.2 1.6 %shard_map.62 = f32[64,128]{1,0:T(8,128)S(1)} custom-call(f32[392,128]{1,0:T(8,128)S(1)} %collective-permute-done.chip_ref, f32[1024,256]{1,0:T(8,128)S(1)} %get-tuple-element.16.sums_ref, f32[192,256]{1,0:T(8,128)S(1)} %get-tuple-element.17.power_ref, bf16[512,256]{1,0:T(8,128)(2,1)S(1)} %get-tuple-element.18.pick_a, ...), custom_call_target="tpu_custom_call" | custom-call | tf_op jit(solution)/shard_map/pallas_call | solution.py:404
  50.8 13.5 %all_to_all.11 = f32[32,2,128]{2,1,0:T(2,128)S(1)} all-to-all(f32[32,2,128]{2,1,0:T(2,128)S(1)} %bitcast.13), channel_id=1, replica_groups=mesh['acq'=32,'az'=8] {'acq'}, dimensions={0} | all-to-all | bytes 65536 | tf_op jit(solution)/shard_map/all_to_all | solution.py:407
  64.4 0.7 %shard_map.63 = (f32[32,64]{1,0:T(8,128)}, f32[32,64]{1,0:T(8,128)}, f32[32,64]{1,0:T(8,128)}) custom-call(f32[64,128]{1,0:T(8,128)S(1)} %bitcast.14), custom_call_target="tpu_custom_call" | custom-call | tf_op jit(solution)/shard_map/pallas_call | solution.py:408
Async XLA Ops:
  39.2 10.0 %collective-permute-start = (f32[392,128]{1,0:T(8,128)S(1)}, f32[392,128]{1,0:T(8,128)S(1)}, u32[]{:S(2)}, u32[]{:S(2)}) collective-permute-start(f32[392,128]{1,0:T(8,128)S(1)} %get-tuple-element.15), channel_id=1, source_target_pairs={{1,2},{3,4},{5,6},{2,1},{4,3},{6,5},{9,10},{11,12},{13,14},{10,9},... | collective-permute-start | bytes 602120 | tf_op jit(solution)/shard_map/ppermute | solution.py:396
  45.3 2.7 %collective-permute-start.1 = (f32[384,128]{1,0:T(8,128)S(1)}, f32[384,128]{1,0:T(8,128)S(1)}, u32[]{:S(2)}, u32[]{:S(2)}) collective-permute-start(f32[384,128]{1,0:T(8,128)S(1)} %get-tuple-element.20), channel_id=1, source_target_pairs={{0,1},{2,3},{4,5},{6,7},{1,0},{3,2},{5,4},{7,6},{8,9},{10,11},{12,... | collective-permute-start | bytes 589832 | tf_op jit(solution)/shard_map/ppermute | solution.py:397

commit v5 on v4

--- a/solution.py
+++ b/solution.py
@@ -147,9 +147,9 @@
     return jnp.concatenate([box, box], axis=0)
 
 
-def choose(pick_a, pick_b, table, picked, at, width):
+def choose(pick_a, pick_b, table, picked, at, width, parts):
     columns = slice(at, at + width)
-    picked[PAIRS:, columns] = dot(pick_b[...], table[:, columns])
+    picked[PAIRS:, columns] = dot(pick_b[:, : parts * K], table[: parts * K, columns])
     for g in range(4):
         few = jnp.concatenate([table[p * K + g * PART : p * K + (g + 1) * PART, columns] for p in range(3)], axis=0)
         picked[128 * g : 128 * (g + 1), columns] = dot(pick_a[128 * g : 128 * (g + 1), : 3 * PART], few)
@@ -194,7 +194,8 @@
 
 
 def enter_power(table, x, box, at):
-    enter(table, dot(jnp.concatenate(pieces_of(x, 2), axis=1), box), at)
+    high, mid, low = pieces_of(x, 3)
+    enter(table, dot(jnp.concatenate([high, mid], axis=1), box) + dot(low, box[:128]), at)
 
 
 def coherence_of(total, picked, top, row, at):
@@ -237,12 +238,12 @@
         for part, x in enumerate(parts):
             enter(table, x, t * 256 + part * 128)
         squares.append(parts[0] * parts[0] + parts[1] * parts[1])
-        choose(pick_a, pick_b, table, picked, t * 256, 256)
+        choose(pick_a, pick_b, table, picked, t * 256, 256, 2)
     sums = own_rows(squares)
     up_power[:, 0:128], up_power[:, 128:256] = sums[0], sums[1]
     down_power[:, 0:128], down_power[:, 128:256] = sums[4], sums[3]
     enter_power(table, sums[2], box, HALF * 256)
-    choose(pick_a, pick_b, table, picked, HALF * 256, 128)
+    choose(pick_a, pick_b, table, picked, HALF * 256, 128, 3)
 
     def rows(top):
         for f, field in enumerate(cross(picked, top, HALF)):
@@ -269,11 +270,11 @@
     parts = [edge_ref[part * ACQ : (part + 1) * ACQ, :] for part in range(2)]
     for part, x in enumerate(parts):
         enter(table, x, part * 128)
-    choose(pick_a, pick_b, table, picked, 0, 256)
+    choose(pick_a, pick_b, table, picked, 0, 256, 2)
     square = parts[0] * parts[0] + parts[1] * parts[1]
     for n, x in enumerate(edge_rows(power_ref[:, 0:128], power_ref[:, 128:256], square, low)):
         enter_power(table, x, box, 256 + n * 128)
-    choose(pick_a, pick_b, table, picked, 256, 256)
+    choose(pick_a, pick_b, table, picked, 256, 256, 3)
 
     def rows(top):
         for f, field in enumerate(cross(picked, top, 1)):

time: 65.6 us -> 65.3 us (level)
  transfers between devices with their start and end apart: 2 -> 2, of which waited for: 0 -> 0; matrix products, arithmetic and copies ran while one was open for 0% -> 0% of each run, Pallas kernels for 6% -> 5%
where the time goes in v5:
time: 65.3 us; the launch traced here: 64.7 us
  blocking collectives  50.2 us (77%)
  Pallas kernels  7.65 us (12%)
  starting transfers between devices  6.18 us (9%)
  between operations  0.69 us (1%)
    all_to_all x1, blocking collectives, per_device(): recv = lax.all_to_all(send, 'acq', split_axis=0, concat_axis=0, tiled=True)  36.6 us
    all_to_all x1, blocking collectives, per_device(): lax.all_to_all(result.reshape(DEVS, 2, 128), 'acq', split_axis=0, concat_...  13.5 us
    ppermute x1, starting transfers between devices, per_device(): chip = lax.ppermute(chip, 'az', across + [(j, i) for i, j in across])  6.08 us
    pallas_call x1, Pallas kernels, per_device(): call(own_kernel, OWN_OUTS, [VMEM], OWN_SCRATCH, cost_estimate=cost[0])(recv)  2.25 us
    pallas_call x1, Pallas kernels, per_device(): call(pack_kernel, f32(DEVS * CHUNK, 128), [HBM] * 3, (((ROWS, ACQ_DEV, RG...  1.74 us
    pallas_call x1, Pallas kernels, per_device(): call(chip_kernel, f32(2 * DEVS, 128), [VMEM] * 6, CHIP_SCRATCH)  1.6 us
  transfers between devices with their start and end apart: 2, of which 0 were waited for; matrix products, arithmetic and copies ran while one was open for 0% of the time, Pallas kernels for 5%

profile of v5, /device:TPU:1, one launch (start us, length us, event | category | flops | bytes accessed | tf_op | source)
XLA Modules:
  0.0 64.7 jit_solution(12346419940009268439)
XLA Ops:
  0.6 1.7 %shard_map.58 = f32[1920,128]{1,0:T(8,128)S(1)} custom-call(f32[10,6,1280]{2,1,0:T(8,128)} %bitcast.15, f32[10,6,1280]{2,1,0:T(8,128)} %bitcast.16, s32[2,16]{1,0:T(2,128)} %bitcast.17), custom_call_target="tpu_custom_call" | custom-call | tf_op jit(solution)/shard_map/pallas_call | solution.py:376
  2.4 36.6 %all_to_all.10 = f32[32,15,4,128]{3,2,1,0:T(4,128)S(1)} all-to-all(f32[32,15,4,128]{3,2,1,0:T(4,128)S(1)} %bitcast.12), channel_id=1, replica_groups=mesh['acq'=32,'az'=8] {'acq'}, dimensions={0} | all-to-all | bytes 1966080 | tf_op jit(solution)/shard_map/all_to_all | solution.py:391
  39.0 0.2 shard_map.59
  39.2 6.1 %collective-permute-start = (f32[392,128]{1,0:T(8,128)S(1)}, f32[392,128]{1,0:T(8,128)S(1)}, u32[]{:S(2)}, u32[]{:S(2)}) collective-permute-start(f32[392,128]{1,0:T(8,128)S(1)} %get-tuple-element.15), channel_id=1, source_target_pairs={{1,2},{3,4},{5,6},{2,1},{4,3},{6,5},{9,10},{11,12},{13,14},{10,9},... | collective-permute-start | bytes 602120 | tf_op jit(solution)/shard_map/ppermute | solution.py:397
  45.3 0.1 collective-permute-start.1
  45.4 2.2 %shard_map.60 = (f32[1024,256]{1,0:T(8,128)S(1)}, f32[1024,256]{1,0:T(8,128)S(1)}, f32[192,256]{1,0:T(8,128)S(1)}, f32[192,256]{1,0:T(8,128)S(1)}, bf16[512,256]...) custom-call(f32[1920,128]{1,0:T(8,128)S(1)} %bitcast.11), custom_call_target="tpu_custom_call" | custom-call | flops 1000 | bytes 1000 | tf_op jit(solution)/shard_map/pallas_call | solution.py:400
  47.6 0.0 collective-permute-done.1.core_ref
  47.6 1.2 %shard_map.61.value_ref = f32[512,128]{1,0:T(8,128)S(1)} custom-call(f32[384,128]{1,0:T(8,128)S(1)} %collective-permute-done.1.core_ref, f32[1024,256]{1,0:T(8,128)S(1)} %get-tuple-element.21.sums_ref, f32[192,256]{1,0:T(8,128)S(1)} %get-tuple-element.22.power_ref, bf16[512,256]{1,0:T(8,128)(2,1)S(1)} %get-tuple-element.18.pick_a, ...), custom_call_target="tpu_custom_call" | custom-call | flops 1000 | bytes 1000 | tf_op jit(solution)/shard_map/pallas_call | solution.py:402
  48.8 0.0 collective-permute-done.chip_ref
  48.8 1.6 %shard_map.62 = f32[64,128]{1,0:T(8,128)S(1)} custom-call(f32[392,128]{1,0:T(8,128)S(1)} %collective-permute-done.chip_ref, f32[1024,256]{1,0:T(8,128)S(1)} %get-tuple-element.16.sums_ref, f32[192,256]{1,0:T(8,128)S(1)} %get-tuple-element.17.power_ref, bf16[512,256]{1,0:T(8,128)(2,1)S(1)} %get-tuple-element.18.pick_a, ...), custom_call_target="tpu_custom_call" | custom-call | tf_op jit(solution)/shard_map/pallas_call | solution.py:405
  50.5 13.5 %all_to_all.11 = f32[32,2,128]{2,1,0:T(2,128)S(1)} all-to-all(f32[32,2,128]{2,1,0:T(2,128)S(1)} %bitcast.13), channel_id=1, replica_groups=mesh['acq'=32,'az'=8] {'acq'}, dimensions={0} | all-to-all | bytes 65536 | tf_op jit(solution)/shard_map/all_to_all | solution.py:408
  64.0 0.7 %shard_map.63 = (f32[32,64]{1,0:T(8,128)}, f32[32,64]{1,0:T(8,128)}, f32[32,64]{1,0:T(8,128)}) custom-call(f32[64,128]{1,0:T(8,128)S(1)} %bitcast.14), custom_call_target="tpu_custom_call" | custom-call | tf_op jit(solution)/shard_map/pallas_call | solution.py:409
Async XLA Ops:
  39.2 9.7 %collective-permute-start = (f32[392,128]{1,0:T(8,128)S(1)}, f32[392,128]{1,0:T(8,128)S(1)}, u32[]{:S(2)}, u32[]{:S(2)}) collective-permute-start(f32[392,128]{1,0:T(8,128)S(1)} %get-tuple-element.15), channel_id=1, source_target_pairs={{1,2},{3,4},{5,6},{2,1},{4,3},{6,5},{9,10},{11,12},{13,14},{10,9},... | collective-permute-start | bytes 602120 | tf_op jit(solution)/shard_map/ppermute | solution.py:397
  45.3 2.4 %collective-permute-start.1 = (f32[384,128]{1,0:T(8,128)S(1)}, f32[384,128]{1,0:T(8,128)S(1)}, u32[]{:S(2)}, u32[]{:S(2)}) collective-permute-start(f32[384,128]{1,0:T(8,128)S(1)} %get-tuple-element.20), channel_id=1, source_target_pairs={{0,1},{2,3},{4,5},{6,7},{1,0},{3,2},{5,4},{7,6},{8,9},{10,11},{12,... | collective-permute-start | bytes 589832 | tf_op jit(solution)/shard_map/ppermute | solution.py:398

commit v6 on v5

--- a/solution.py
+++ b/solution.py
@@ -270,10 +270,10 @@
     parts = [edge_ref[part * ACQ : (part + 1) * ACQ, :] for part in range(2)]
     for part, x in enumerate(parts):
         enter(table, x, part * 128)
-    choose(pick_a, pick_b, table, picked, 0, 256, 2)
     square = parts[0] * parts[0] + parts[1] * parts[1]
     for n, x in enumerate(edge_rows(power_ref[:, 0:128], power_ref[:, 128:256], square, low)):
         enter_power(table, x, box, 256 + n * 128)
+    choose(pick_a, pick_b, table, picked, 0, 256, 2)
     choose(pick_a, pick_b, table, picked, 256, 256, 3)
 
     def rows(top):

time: 65.3 us -> 65.2 us (level)
  no operation moved by 1% of the time
where the time goes in v6:
time: 65.2 us; the launch traced here: 64.5 us
  blocking collectives  50.2 us (77%)
  Pallas kernels  7.51 us (12%)
  starting transfers between devices  6.18 us (9%)
  between operations  0.7 us (1%)
    all_to_all x1, blocking collectives, per_device(): recv = lax.all_to_all(send, 'acq', split_axis=0, concat_axis=0, tiled=True)  36.6 us
    all_to_all x1, blocking collectives, per_device(): lax.all_to_all(result.reshape(DEVS, 2, 128), 'acq', split_axis=0, concat_...  13.5 us
    ppermute x1, starting transfers between devices, per_device(): chip = lax.ppermute(chip, 'az', across + [(j, i) for i, j in across])  6.08 us
    pallas_call x1, Pallas kernels, per_device(): call(own_kernel, OWN_OUTS, [VMEM], OWN_SCRATCH, cost_estimate=cost[0])(recv)  2.25 us
    pallas_call x1, Pallas kernels, per_device(): call(pack_kernel, f32(DEVS * CHUNK, 128), [HBM] * 3, (((ROWS, ACQ_DEV, RG...  1.74 us
    pallas_call x1, Pallas kernels, per_device(): call(chip_kernel, f32(2 * DEVS, 128), [VMEM] * 6, CHIP_SCRATCH)  1.54 us
  transfers between devices with their start and end apart: 2, of which 0 were waited for; matrix products, arithmetic and copies ran while one was open for 0% of the time, Pallas kernels for 5%

profile of v6, /device:TPU:1, one launch (start us, length us, event | category | flops | bytes accessed | tf_op | source)
XLA Modules:
  0.0 64.5 jit_solution(11265153858492846484)
XLA Ops:
  0.6 1.7 %shard_map.58 = f32[1920,128]{1,0:T(8,128)S(1)} custom-call(f32[10,6,1280]{2,1,0:T(8,128)} %bitcast.15, f32[10,6,1280]{2,1,0:T(8,128)} %bitcast.16, s32[2,16]{1,0:T(2,128)} %bitcast.17), custom_call_target="tpu_custom_call" | custom-call | tf_op jit(solution)/shard_map/pallas_call | solution.py:376
  2.4 36.6 %all_to_all.10 = f32[32,15,4,128]{3,2,1,0:T(4,128)S(1)} all-to-all(f32[32,15,4,128]{3,2,1,0:T(4,128)S(1)} %bitcast.12), channel_id=1, replica_groups=mesh['acq'=32,'az'=8] {'acq'}, dimensions={0} | all-to-all | bytes 1966080 | tf_op jit(solution)/shard_map/all_to_all | solution.py:391
  39.0 0.2 shard_map.59
  39.2 6.1 %collective-permute-start = (f32[392,128]{1,0:T(8,128)S(1)}, f32[392,128]{1,0:T(8,128)S(1)}, u32[]{:S(2)}, u32[]{:S(2)}) collective-permute-start(f32[392,128]{1,0:T(8,128)S(1)} %get-tuple-element.15), channel_id=1, source_target_pairs={{1,2},{3,4},{5,6},{2,1},{4,3},{6,5},{9,10},{11,12},{13,14},{10,9},... | collective-permute-start | bytes 602120 | tf_op jit(solution)/shard_map/ppermute | solution.py:397
  45.3 0.1 collective-permute-start.1
  45.4 2.2 %shard_map.60 = (f32[1024,256]{1,0:T(8,128)S(1)}, f32[1024,256]{1,0:T(8,128)S(1)}, f32[192,256]{1,0:T(8,128)S(1)}, f32[192,256]{1,0:T(8,128)S(1)}, bf16[512,256]...) custom-call(f32[1920,128]{1,0:T(8,128)S(1)} %bitcast.11), custom_call_target="tpu_custom_call" | custom-call | flops 1000 | bytes 1000 | tf_op jit(solution)/shard_map/pallas_call | solution.py:400
  47.6 0.0 collective-permute-done.1.core_ref
  47.6 1.1 %shard_map.61.value_ref = f32[512,128]{1,0:T(8,128)S(1)} custom-call(f32[384,128]{1,0:T(8,128)S(1)} %collective-permute-done.1.core_ref, f32[1024,256]{1,0:T(8,128)S(1)} %get-tuple-element.21.sums_ref, f32[192,256]{1,0:T(8,128)S(1)} %get-tuple-element.22.power_ref, bf16[512,256]{1,0:T(8,128)(2,1)S(1)} %get-tuple-element.18.pick_a, ...), custom_call_target="tpu_custom_call" | custom-call | flops 1000 | bytes 1000 | tf_op jit(solution)/shard_map/pallas_call | solution.py:402
  48.8 0.0 collective-permute-done.chip_ref
  48.8 1.5 %shard_map.62 = f32[64,128]{1,0:T(8,128)S(1)} custom-call(f32[392,128]{1,0:T(8,128)S(1)} %collective-permute-done.chip_ref, f32[1024,256]{1,0:T(8,128)S(1)} %get-tuple-element.16.sums_ref, f32[192,256]{1,0:T(8,128)S(1)} %get-tuple-element.17.power_ref, bf16[512,256]{1,0:T(8,128)(2,1)S(1)} %get-tuple-element.18.pick_a, ...), custom_call_target="tpu_custom_call" | custom-call | tf_op jit(solution)/shard_map/pallas_call | solution.py:405
  50.3 13.5 %all_to_all.11 = f32[32,2,128]{2,1,0:T(2,128)S(1)} all-to-all(f32[32,2,128]{2,1,0:T(2,128)S(1)} %bitcast.13), channel_id=1, replica_groups=mesh['acq'=32,'az'=8] {'acq'}, dimensions={0} | all-to-all | bytes 65536 | tf_op jit(solution)/shard_map/all_to_all | solution.py:408
  63.8 0.7 %shard_map.63 = (f32[32,64]{1,0:T(8,128)}, f32[32,64]{1,0:T(8,128)}, f32[32,64]{1,0:T(8,128)}) custom-call(f32[64,128]{1,0:T(8,128)S(1)} %bitcast.14), custom_call_target="tpu_custom_call" | custom-call | tf_op jit(solution)/shard_map/pallas_call | solution.py:409
Async XLA Ops:
  39.2 9.6 %collective-permute-start = (f32[392,128]{1,0:T(8,128)S(1)}, f32[392,128]{1,0:T(8,128)S(1)}, u32[]{:S(2)}, u32[]{:S(2)}) collective-permute-start(f32[392,128]{1,0:T(8,128)S(1)} %get-tuple-element.15), channel_id=1, source_target_pairs={{1,2},{3,4},{5,6},{2,1},{4,3},{6,5},{9,10},{11,12},{13,14},{10,9},... | collective-permute-start | bytes 602120 | tf_op jit(solution)/shard_map/ppermute | solution.py:397
  45.3 2.4 %collective-permute-start.1 = (f32[384,128]{1,0:T(8,128)S(1)}, f32[384,128]{1,0:T(8,128)S(1)}, u32[]{:S(2)}, u32[]{:S(2)}) collective-permute-start(f32[384,128]{1,0:T(8,128)S(1)} %get-tuple-element.20), channel_id=1, source_target_pairs={{0,1},{2,3},{4,5},{6,7},{1,0},{3,2},{5,4},{7,6},{8,9},{10,11},{12,... | collective-permute-start | bytes 589832 | tf_op jit(solution)/shard_map/ppermute | solution.py:398

commit v7 on v6

--- a/solution.py
+++ b/solution.py
@@ -174,18 +174,14 @@
     next_two = next_one + pltpu.roll(jnp.where(low, v3, v1), 64, 1)
     v12, v34 = v1 + v2, v3 + v4
     v012, v234 = v0 + v12, v2 + v34
-    return [
-        v012 + jnp.where(low, 0.0, next_two),
-        (v012 + v3) + jnp.where(low, 0.0, next_one),
-        v012 + v34,
-        (v1 + v234) + jnp.where(low, next_one, 0.0),
-        v234 + jnp.where(low, next_two, 0.0),
-    ]
-
-
-def edge_rows(near, far, edge, low):
+    return v012, v012 + v3, v012 + v34, v1 + v234, v234, next_two, next_one
+
+
+def edge_rows(sums, turned, here, edge, low):
     inside = (lanes_of(edge.shape) < 64) == low
-    return near + jnp.where(inside, edge + pltpu.roll(edge, 64, 1), 0.0), far + jnp.where(inside, edge, 0.0)
+    two = edge + pltpu.roll(edge, 64, 1)
+    near = sums[here, 0:128] + jnp.where(inside, two, turned[here, 0:128])
+    return near, sums[here, 128:256] + jnp.where(inside, edge, turned[here, 128:256])
 
 
 def store_terms(terms, top, x):
@@ -217,7 +213,7 @@
 
 
 def own_kernel(
-    recv_ref, up_ref, down_ref, up_power, down_power, pick_a, pick_b, value_ref, table, picked, terms, total
+    recv_ref, up_ref, down_ref, turn_ref, up_power, down_power, turn_power, pick_a, pick_b, value_ref, table, picked, terms, total
 ):
     lane = lanes_of((128, K))
     few = lane - PART * ((lane * 342) >> 14)
@@ -242,6 +238,7 @@
     sums = own_rows(squares)
     up_power[:, 0:128], up_power[:, 128:256] = sums[0], sums[1]
     down_power[:, 0:128], down_power[:, 128:256] = sums[4], sums[3]
+    turn_power[:, 0:128], turn_power[:, 128:256] = sums[5], sums[6]
     enter_power(table, sums[2], box, HALF * 256)
     choose(pick_a, pick_b, table, picked, HALF * 256, 128, 3)
 
@@ -251,6 +248,7 @@
             here = pl.ds(top + f * PAIRS, 16)
             up_ref[here, 0:128], up_ref[here, 128:256] = x[0], x[1]
             down_ref[here, 0:128], down_ref[here, 128:256] = x[4], x[3]
+            turn_ref[here, 0:128], turn_ref[here, 128:256] = x[5], x[6]
             store_terms(terms, top + f * PAIRS, x[2])
 
     for_pairs(rows)
@@ -264,14 +262,14 @@
     for_pairs(some)
 
 
-def edge_coherence(edge_ref, sums_ref, power_ref, pick_a, pick_b, table, picked, terms, total, low):
+def edge_coherence(edge_ref, sums, powers, pick_a, pick_b, table, picked, terms, total, low):
     fill(table)
     box = along_range()
     parts = [edge_ref[part * ACQ : (part + 1) * ACQ, :] for part in range(2)]
     for part, x in enumerate(parts):
         enter(table, x, part * 128)
     square = parts[0] * parts[0] + parts[1] * parts[1]
-    for n, x in enumerate(edge_rows(power_ref[:, 0:128], power_ref[:, 128:256], square, low)):
+    for n, x in enumerate(edge_rows(*powers, slice(0, ACQ), square, low)):
         enter_power(table, x, box, 256 + n * 128)
     choose(pick_a, pick_b, table, picked, 0, 256, 2)
     choose(pick_a, pick_b, table, picked, 256, 256, 3)
@@ -279,7 +277,7 @@
     def rows(top):
         for f, field in enumerate(cross(picked, top, 1)):
             here = pl.ds(top + f * PAIRS, 16)
-            for n, x in enumerate(edge_rows(sums_ref[here, 0:128], sums_ref[here, 128:256], field[0], low)):
+            for n, x in enumerate(edge_rows(*sums, here, field[0], low)):
                 store_terms(terms, top + (2 * n + f) * PAIRS, x)
 
     for_pairs(rows)
@@ -291,8 +289,9 @@
     return value_ref[pl.ds(top, 16), :] + jnp.where((lanes_of(size.shape) & 63) < STEP, size, 0.0)
 
 
-def core_kernel(core_ref, sums_ref, power_ref, pick_a, pick_b, value_ref, out_ref, table, picked, terms, total):
-    edge_coherence(core_ref, sums_ref, power_ref, pick_a, pick_b, table, picked, terms, total, False)
+def core_kernel(core_ref, sums_ref, turn_ref, power_ref, turn_power, pick_a, pick_b, value_ref, out_ref, table, picked, terms, total):
+    sums, powers = (sums_ref, turn_ref), (power_ref, turn_power)
+    edge_coherence(core_ref, sums, powers, pick_a, pick_b, table, picked, terms, total, False)
 
     def some(top):
         out_ref[pl.ds(top, 16), :] = edge_value(value_ref, total, picked, top)
@@ -300,8 +299,9 @@
     for_pairs(some)
 
 
-def chip_kernel(chip_ref, sums_ref, power_ref, pick_a, pick_b, value_ref, out_ref, table, picked, terms, total, ends):
-    edge_coherence(chip_ref, sums_ref, power_ref, pick_a, pick_b, table, picked, terms, total, True)
+def chip_kernel(chip_ref, sums_ref, turn_ref, power_ref, turn_power, pick_a, pick_b, value_ref, out_ref, table, picked, terms, total, ends):
+    sums, powers = (sums_ref, turn_ref), (power_ref, turn_power)
+    edge_coherence(chip_ref, sums, powers, pick_a, pick_b, table, picked, terms, total, True)
 
     def some(top):
         for p, piece in enumerate(pieces_of(edge_value(value_ref, total, picked, top), 3)):
@@ -355,7 +355,7 @@
     return jax.ShapeDtypeStruct(shape, BF16)
 
 
-EDGE_OUTS = (f32(2 * PAIRS, 256),) * 2 + (f32(ACQ, 256),) * 2
+EDGE_OUTS = (f32(2 * PAIRS, 256),) * 3 + (f32(ACQ, 256),) * 3
 OWN_OUTS = EDGE_OUTS + (bf16(PAIRS, K), bf16(PAIRS, 3 * K), f32(PAIRS, 128))
 OWN_SCRATCH = (
     ((3 * K, HALF * 256 + 128), BF16),
@@ -398,12 +398,12 @@
     core = lax.ppermute(core, "az", inside + [(j, i) for i, j in inside])
     cost = [pl.CostEstimate(flops=n, bytes_accessed=n, transcendentals=0) for n in (10**3, 10**3)]
     own = call(own_kernel, OWN_OUTS, [VMEM], OWN_SCRATCH, cost_estimate=cost[0])(recv)
-    up, down, up_power, down_power, pick_a, pick_b, value = own
-    value = call(core_kernel, f32(PAIRS, 128), [VMEM] * 6, EDGE_SCRATCH, cost_estimate=cost[1])(
-        core, down, down_power, pick_a, pick_b, value
+    up, down, turn, up_power, down_power, turn_power, pick_a, pick_b, value = own
+    value = call(core_kernel, f32(PAIRS, 128), [VMEM] * 8, EDGE_SCRATCH, cost_estimate=cost[1])(
+        core, down, turn, down_power, turn_power, pick_a, pick_b, value
     )
-    result = call(chip_kernel, f32(2 * DEVS, 128), [VMEM] * 6, CHIP_SCRATCH)(
-        chip, up, up_power, pick_a, pick_b, value
+    result = call(chip_kernel, f32(2 * DEVS, 128), [VMEM] * 8, CHIP_SCRATCH)(
+        chip, up, turn, up_power, turn_power, pick_a, pick_b, value
     )
     got = lax.all_to_all(result.reshape(DEVS, 2, 128), "acq", split_axis=0, concat_axis=0, tiled=True)
     outs = call(finish_kernel, (f32(32, 64),) * 3, [VMEM])(got.reshape(2 * DEVS, 128))

time: 65.2 us -> 65.2 us (level)
  no operation moved by 1% of the time
where the time goes in v7:
time: 65.2 us; the launch traced here: 64.5 us
  blocking collectives  50.1 us (77%)
  Pallas kernels  7.43 us (11%)
  starting transfers between devices  6.18 us (9%)
  between operations  0.69 us (1%)
    all_to_all x1, blocking collectives, per_device(): recv = lax.all_to_all(send, 'acq', split_axis=0, concat_axis=0, tiled=True)  36.6 us
    all_to_all x1, blocking collectives, per_device(): lax.all_to_all(result.reshape(DEVS, 2, 128), 'acq', split_axis=0, concat_...  13.5 us
    ppermute x1, starting transfers between devices, per_device(): chip = lax.ppermute(chip, 'az', across + [(j, i) for i, j in across])  6.08 us
    pallas_call x1, Pallas kernels, per_device(): call(own_kernel, OWN_OUTS, [VMEM], OWN_SCRATCH, cost_estimate=cost[0])(recv)  2.19 us
    pallas_call x1, Pallas kernels, per_device(): call(pack_kernel, f32(DEVS * CHUNK, 128), [HBM] * 3, (((ROWS, ACQ_DEV, RG...  1.74 us
    pallas_call x1, Pallas kernels, per_device(): call(chip_kernel, f32(2 * DEVS, 128), [VMEM] * 8, CHIP_SCRATCH)  1.53 us
  transfers between devices with their start and end apart: 2, of which 0 were waited for; matrix products, arithmetic and copies ran while one was open for 0% of the time, Pallas kernels for 5%

profile of v7, /device:TPU:1, one launch (start us, length us, event | category | flops | bytes accessed | tf_op | source)
XLA Modules:
  0.0 64.5 jit_solution(6157780733565908372)
XLA Ops:
  0.6 1.7 %shard_map.58 = f32[1920,128]{1,0:T(8,128)S(1)} custom-call(f32[10,6,1280]{2,1,0:T(8,128)} %bitcast.15, f32[10,6,1280]{2,1,0:T(8,128)} %bitcast.16, s32[2,16]{1,0:T(2,128)} %bitcast.17), custom_call_target="tpu_custom_call" | custom-call | tf_op jit(solution)/shard_map/pallas_call | solution.py:376
  2.4 36.6 %all_to_all.10 = f32[32,15,4,128]{3,2,1,0:T(4,128)S(1)} all-to-all(f32[32,15,4,128]{3,2,1,0:T(4,128)S(1)} %bitcast.12), channel_id=1, replica_groups=mesh['acq'=32,'az'=8] {'acq'}, dimensions={0} | all-to-all | bytes 1966080 | tf_op jit(solution)/shard_map/all_to_all | solution.py:391
  39.0 0.2 shard_map.59
  39.2 6.1 %collective-permute-start = (f32[392,128]{1,0:T(8,128)S(1)}, f32[392,128]{1,0:T(8,128)S(1)}, u32[]{:S(2)}, u32[]{:S(2)}) collective-permute-start(f32[392,128]{1,0:T(8,128)S(1)} %get-tuple-element.17), channel_id=1, source_target_pairs={{1,2},{3,4},{5,6},{2,1},{4,3},{6,5},{9,10},{11,12},{13,14},{10,9},... | collective-permute-start | bytes 602120 | tf_op jit(solution)/shard_map/ppermute | solution.py:397
  45.3 0.1 collective-permute-start.1
  45.4 2.2 %shard_map.60 = (f32[1024,256]{1,0:T(8,128)S(1)}, f32[1024,256]{1,0:T(8,128)S(1)}, f32[1024,256]{1,0:T(8,128)S(1)}, f32[192,256]{1,0:T(8,128)S(1)}, f32[192,256]...) custom-call(f32[1920,128]{1,0:T(8,128)S(1)} %bitcast.11), custom_call_target="tpu_custom_call" | custom-call | flops 1000 | bytes 1000 | tf_op jit(solution)/shard_map/pallas_call | solution.py:400
  47.6 0.0 collective-permute-done.1.core_ref
  47.6 1.1 %shard_map.61.value_ref = f32[512,128]{1,0:T(8,128)S(1)} custom-call(f32[384,128]{1,0:T(8,128)S(1)} %collective-permute-done.1.core_ref, f32[1024,256]{1,0:T(8,128)S(1)} %get-tuple-element.25.sums_ref, f32[1024,256]{1,0:T(8,128)S(1)} %get-tuple-element.19.turn_ref, f32[192,256]{1,0:T(8,128)S(1)} %get-tuple-element.26.power_ref, ...), custom_call_target="tpu_custom_call" | custom-call | flops 1000 | bytes 1000 | tf_op jit(solution)/shard_map/pallas_call | solution.py:402
  48.7 0.0 collective-permute-done.chip_ref
  48.7 1.5 %shard_map.62 = f32[64,128]{1,0:T(8,128)S(1)} custom-call(f32[392,128]{1,0:T(8,128)S(1)} %collective-permute-done.chip_ref, f32[1024,256]{1,0:T(8,128)S(1)} %get-tuple-element.18.sums_ref, f32[1024,256]{1,0:T(8,128)S(1)} %get-tuple-element.19.turn_ref, f32[192,256]{1,0:T(8,128)S(1)} %get-tuple-element.20.power_ref, ...), custom_call_target="tpu_custom_call" | custom-call | tf_op jit(solution)/shard_map/pallas_call | solution.py:405
  50.2 13.5 %all_to_all.11 = f32[32,2,128]{2,1,0:T(2,128)S(1)} all-to-all(f32[32,2,128]{2,1,0:T(2,128)S(1)} %bitcast.13), channel_id=1, replica_groups=mesh['acq'=32,'az'=8] {'acq'}, dimensions={0} | all-to-all | bytes 65536 | tf_op jit(solution)/shard_map/all_to_all | solution.py:408
  63.8 0.7 %shard_map.63 = (f32[32,64]{1,0:T(8,128)}, f32[32,64]{1,0:T(8,128)}, f32[32,64]{1,0:T(8,128)}) custom-call(f32[64,128]{1,0:T(8,128)S(1)} %bitcast.14), custom_call_target="tpu_custom_call" | custom-call | tf_op jit(solution)/shard_map/pallas_call | solution.py:409
Async XLA Ops:
  39.2 9.5 %collective-permute-start = (f32[392,128]{1,0:T(8,128)S(1)}, f32[392,128]{1,0:T(8,128)S(1)}, u32[]{:S(2)}, u32[]{:S(2)}) collective-permute-start(f32[392,128]{1,0:T(8,128)S(1)} %get-tuple-element.17), channel_id=1, source_target_pairs={{1,2},{3,4},{5,6},{2,1},{4,3},{6,5},{9,10},{11,12},{13,14},{10,9},... | collective-permute-start | bytes 602120 | tf_op jit(solution)/shard_map/ppermute | solution.py:397
  45.3 2.3 %collective-permute-start.1 = (f32[384,128]{1,0:T(8,128)S(1)}, f32[384,128]{1,0:T(8,128)S(1)}, u32[]{:S(2)}, u32[]{:S(2)}) collective-permute-start(f32[384,128]{1,0:T(8,128)S(1)} %get-tuple-element.24), channel_id=1, source_target_pairs={{0,1},{2,3},{4,5},{6,7},{1,0},{3,2},{5,4},{7,6},{8,9},{10,11},{12,... | collective-permute-start | bytes 589832 | tf_op jit(solution)/shard_map/ppermute | solution.py:398

commit v8 on v7

--- a/solution.py
+++ b/solution.py
@@ -42,7 +42,7 @@
     for copy in copies:
         copy.start()
     lane = lanes_of((ACQ_DEV, 128))
-    wide = lanes_of((PAIR_DEV, 128))
+    wide = lanes_of((3 * ACQ_DEV, 128))
     copies[0].wait()
     acq = pairs_ref[...]
     group = (acq * 171) >> 10
@@ -55,7 +55,10 @@
         jnp.sum(jnp.where(diagonal, jnp.broadcast_to(index[w : w + 1, :], square), 0.0), axis=1, keepdims=True)
         for w in range(2)
     ]
-    first, second = [jnp.broadcast_to(column, (PAIR_DEV, 128)) for column in columns]
+    none = jnp.zeros((3 * ACQ_DEV - PAIR_DEV, 128), F32)
+    first, second = [jnp.concatenate([jnp.broadcast_to(x, (PAIR_DEV, 128)), none], axis=0) for x in columns]
+    marks = jnp.where(wide == 60, first, jnp.where(wide == 61, second, 0.0))
+    marks = [marks[n * ACQ_DEV : (n + 1) * ACQ_DEV] for n in range(3)]
     tiles = RG // 128
     for part, ref in enumerate((re_ref, im_ref)):
         copies[1 + part].wait()
@@ -83,10 +86,10 @@
                     at = slice(t * 128, (t + 1) * 128)
                     mixed = jnp.where(mask, later[part * HALF + r, :, at] if shifted else ref[row, :, at], mixed)
                 top = d * CHUNK + (part * HALF + r) * ACQ_DEV
-                chunks[top : top + ACQ_DEV, :] = pltpu.roll(mixed, 128 - off, 1) if off else mixed
-        head = chunks[d * CHUNK : d * CHUNK + PAIR_DEV, :]
-        head = jnp.where(wide == 60, first, jnp.where(wide == 61, second, head))
-        chunks[d * CHUNK : d * CHUNK + PAIR_DEV, :] = head
+                mixed = pltpu.roll(mixed, 128 - off, 1) if off else mixed
+                if part == 0 and r < 3:
+                    mixed = mixed + marks[r]
+                chunks[top : top + ACQ_DEV, :] = mixed
 
 
 def acq_rows(recv_ref, part, r):
@@ -97,14 +100,19 @@
     )
 
 
-def edges_kernel(recv_ref, chip_ref, core_ref):
+def chip_edge_kernel(recv_ref, out_ref):
     lane = lanes_of((ACQ, 128))
     for part in range(2):
-        v0, v1, v3, v4 = [acq_rows(recv_ref, part, r) for r in (0, 1, 3, 4)]
-        rows = slice(part * ACQ, (part + 1) * ACQ)
-        chip_ref[rows, :] = jnp.where(lane < 64, v0, pltpu.roll(v1, 64, 1))
-        core_ref[rows, :] = jnp.where(lane < 64, pltpu.roll(v3, 64, 1), v4)
-    chip_ref[2 * ACQ :, :] = jnp.zeros((8, 128), F32)
+        v0, v1 = [acq_rows(recv_ref, part, r) for r in (0, 1)]
+        out_ref[part * ACQ : (part + 1) * ACQ, :] = jnp.where(lane < 64, v0, pltpu.roll(v1, 64, 1))
+    out_ref[2 * ACQ :, :] = jnp.zeros((8, 128), F32)
+
+
+def core_edge_kernel(recv_ref, out_ref):
+    lane = lanes_of((ACQ, 128))
+    for part in range(2):
+        v3, v4 = [acq_rows(recv_ref, part, r) for r in (3, 4)]
+        out_ref[part * ACQ : (part + 1) * ACQ, :] = jnp.where(lane < 64, pltpu.roll(v3, 64, 1), v4)
 
 
 def pieces_of(x, count):
@@ -390,7 +398,8 @@
     send = send.reshape(DEVS, CHUNK // 4, 4, 128)
     recv = lax.all_to_all(send, "acq", split_axis=0, concat_axis=0, tiled=True)
     recv = recv.reshape(DEVS * CHUNK, 128)
-    chip, core = call(edges_kernel, (f32(2 * ACQ + 8, 128), f32(2 * ACQ, 128)), [VMEM])(recv)
+    chip = call(chip_edge_kernel, f32(2 * ACQ + 8, 128), [VMEM])(recv)
+    core = call(core_edge_kernel, f32(2 * ACQ, 128), [VMEM])(recv)
     count = lax.axis_size("az")
     across = [(i, i + 1) for i in range(1, count - 1, 2)]
     inside = [(i, i + 1) for i in range(0, count, 2)]

time: 65.2 us -> 65 us (level)
  no operation moved by 1% of the time
where the time goes in v8:
time: 65 us; the launch traced here: 64.5 us
  blocking collectives  50.2 us (77%)
  Pallas kernels  7.44 us (11%)
  starting transfers between devices  6.17 us (9%)
  between operations  0.7 us (1%)
    all_to_all x1, blocking collectives, per_device(): recv = lax.all_to_all(send, 'acq', split_axis=0, concat_axis=0, tiled=True)  36.6 us
    all_to_all x1, blocking collectives, per_device(): lax.all_to_all(result.reshape(DEVS, 2, 128), 'acq', split_axis=0, concat_...  13.5 us
    ppermute x1, starting transfers between devices, per_device(): chip = lax.ppermute(chip, 'az', across + [(j, i) for i, j in across])  6.07 us
    pallas_call x1, Pallas kernels, per_device(): call(own_kernel, OWN_OUTS, [VMEM], OWN_SCRATCH, cost_estimate=cost[0])(recv)  2.18 us
    pallas_call x1, Pallas kernels, per_device(): call(pack_kernel, f32(DEVS * CHUNK, 128), [HBM] * 3, (((ROWS, ACQ_DEV, RG...  1.68 us
    pallas_call x1, Pallas kernels, per_device(): call(chip_kernel, f32(2 * DEVS, 128), [VMEM] * 8, CHIP_SCRATCH)  1.53 us
  transfers between devices with their start and end apart: 2, of which 0 were waited for; matrix products, arithmetic and copies ran while one was open for 0% of the time, Pallas kernels for 5%

profile of v8, /device:TPU:1, one launch (start us, length us, event | category | flops | bytes accessed | tf_op | source)
XLA Modules:
  0.0 64.5 jit_solution(888803164152398689)
XLA Ops:
  0.6 1.7 %shard_map.58 = f32[1920,128]{1,0:T(8,128)S(1)} custom-call(f32[10,6,1280]{2,1,0:T(8,128)} %bitcast.16, f32[10,6,1280]{2,1,0:T(8,128)} %bitcast.17, s32[2,16]{1,0:T(2,128)} %bitcast.18), custom_call_target="tpu_custom_call" | custom-call | tf_op jit(solution)/shard_map/pallas_call | solution.py:384
  2.3 36.6 %all_to_all.10 = f32[32,15,4,128]{3,2,1,0:T(4,128)S(1)} all-to-all(f32[32,15,4,128]{3,2,1,0:T(4,128)S(1)} %bitcast.13), channel_id=1, replica_groups=mesh['acq'=32,'az'=8] {'acq'}, dimensions={0} | all-to-all | bytes 1966080 | tf_op jit(solution)/shard_map/all_to_all | solution.py:399
  39.0 0.1 shard_map.59
  39.1 6.1 %collective-permute-start = (f32[392,128]{1,0:T(8,128)S(1)}, f32[392,128]{1,0:T(8,128)S(1)}, u32[]{:S(2)}, u32[]{:S(2)}) collective-permute-start(f32[392,128]{1,0:T(8,128)S(1)} %shard_map.59), channel_id=1, source_target_pairs={{1,2},{3,4},{5,6},{2,1},{4,3},{6,5},{9,10},{11,12},{13,14},{10,9},... | collective-permute-start | bytes 602120 | tf_op jit(solution)/shard_map/ppermute | solution.py:406
  45.2 0.1 shard_map.61
  45.3 0.1 collective-permute-start.1
  45.4 2.2 %shard_map.60 = (f32[1024,256]{1,0:T(8,128)S(1)}, f32[1024,256]{1,0:T(8,128)S(1)}, f32[1024,256]{1,0:T(8,128)S(1)}, f32[192,256]{1,0:T(8,128)S(1)}, f32[192,256]...) custom-call(f32[1920,128]{1,0:T(8,128)S(1)} %bitcast.12), custom_call_target="tpu_custom_call" | custom-call | flops 1000 | bytes 1000 | tf_op jit(solution)/shard_map/pallas_call | solution.py:409
  47.6 0.0 collective-permute-done.1.core_ref
  47.6 1.1 %shard_map.62.value_ref = f32[512,128]{1,0:T(8,128)S(1)} custom-call(f32[384,128]{1,0:T(8,128)S(1)} %collective-permute-done.1.core_ref, f32[1024,256]{1,0:T(8,128)S(1)} %get-tuple-element.21.sums_ref, f32[1024,256]{1,0:T(8,128)S(1)} %get-tuple-element.16.turn_ref, f32[192,256]{1,0:T(8,128)S(1)} %get-tuple-element.22.power_ref, ...), custom_call_target="tpu_custom_call" | custom-call | flops 1000 | bytes 1000 | tf_op jit(solution)/shard_map/pallas_call | solution.py:411
  48.7 0.0 collective-permute-done.chip_ref
  48.7 1.5 %shard_map.63 = f32[64,128]{1,0:T(8,128)S(1)} custom-call(f32[392,128]{1,0:T(8,128)S(1)} %collective-permute-done.chip_ref, f32[1024,256]{1,0:T(8,128)S(1)} %get-tuple-element.15.sums_ref, f32[1024,256]{1,0:T(8,128)S(1)} %get-tuple-element.16.turn_ref, f32[192,256]{1,0:T(8,128)S(1)} %get-tuple-element.17.power_ref, ...), custom_call_target="tpu_custom_call" | custom-call | tf_op jit(solution)/shard_map/pallas_call | solution.py:414
  50.3 13.5 %all_to_all.11 = f32[32,2,128]{2,1,0:T(2,128)S(1)} all-to-all(f32[32,2,128]{2,1,0:T(2,128)S(1)} %bitcast.14), channel_id=1, replica_groups=mesh['acq'=32,'az'=8] {'acq'}, dimensions={0} | all-to-all | bytes 65536 | tf_op jit(solution)/shard_map/all_to_all | solution.py:417
  63.8 0.7 %shard_map.64 = (f32[32,64]{1,0:T(8,128)}, f32[32,64]{1,0:T(8,128)}, f32[32,64]{1,0:T(8,128)}) custom-call(f32[64,128]{1,0:T(8,128)S(1)} %bitcast.15), custom_call_target="tpu_custom_call" | custom-call | tf_op jit(solution)/shard_map/pallas_call | solution.py:418
Async XLA Ops:
  39.1 9.6 %collective-permute-start = (f32[392,128]{1,0:T(8,128)S(1)}, f32[392,128]{1,0:T(8,128)S(1)}, u32[]{:S(2)}, u32[]{:S(2)}) collective-permute-start(f32[392,128]{1,0:T(8,128)S(1)} %shard_map.59), channel_id=1, source_target_pairs={{1,2},{3,4},{5,6},{2,1},{4,3},{6,5},{9,10},{11,12},{13,14},{10,9},... | collective-permute-start | bytes 602120 | tf_op jit(solution)/shard_map/ppermute | solution.py:406
  45.3 2.3 %collective-permute-start.1 = (f32[384,128]{1,0:T(8,128)S(1)}, f32[384,128]{1,0:T(8,128)S(1)}, u32[]{:S(2)}, u32[]{:S(2)}) collective-permute-start(f32[384,128]{1,0:T(8,128)S(1)} %shard_map.61), channel_id=1, source_target_pairs={{0,1},{2,3},{4,5},{6,7},{1,0},{3,2},{5,4},{7,6},{8,9},{10,11},{12,... | collective-permute-start | bytes 589832 | tf_op jit(solution)/shard_map/ppermute | solution.py:407

commit v9 on v6

--- a/solution.py
+++ b/solution.py
@@ -42,7 +42,7 @@
     for copy in copies:
         copy.start()
     lane = lanes_of((ACQ_DEV, 128))
-    wide = lanes_of((PAIR_DEV, 128))
+    wide = lanes_of((3 * ACQ_DEV, 128))
     copies[0].wait()
     acq = pairs_ref[...]
     group = (acq * 171) >> 10
@@ -55,7 +55,10 @@
         jnp.sum(jnp.where(diagonal, jnp.broadcast_to(index[w : w + 1, :], square), 0.0), axis=1, keepdims=True)
         for w in range(2)
     ]
-    first, second = [jnp.broadcast_to(column, (PAIR_DEV, 128)) for column in columns]
+    none = jnp.zeros((3 * ACQ_DEV - PAIR_DEV, 128), F32)
+    first, second = [jnp.concatenate([jnp.broadcast_to(x, (PAIR_DEV, 128)), none], axis=0) for x in columns]
+    marks = jnp.where(wide == 60, first, jnp.where(wide == 61, second, 0.0))
+    marks = [marks[n * ACQ_DEV : (n + 1) * ACQ_DEV] for n in range(3)]
     tiles = RG // 128
     for part, ref in enumerate((re_ref, im_ref)):
         copies[1 + part].wait()
@@ -83,10 +86,10 @@
                     at = slice(t * 128, (t + 1) * 128)
                     mixed = jnp.where(mask, later[part * HALF + r, :, at] if shifted else ref[row, :, at], mixed)
                 top = d * CHUNK + (part * HALF + r) * ACQ_DEV
-                chunks[top : top + ACQ_DEV, :] = pltpu.roll(mixed, 128 - off, 1) if off else mixed
-        head = chunks[d * CHUNK : d * CHUNK + PAIR_DEV, :]
-        head = jnp.where(wide == 60, first, jnp.where(wide == 61, second, head))
-        chunks[d * CHUNK : d * CHUNK + PAIR_DEV, :] = head
+                mixed = pltpu.roll(mixed, 128 - off, 1) if off else mixed
+                if part == 0 and r < 3:
+                    mixed = mixed + marks[r]
+                chunks[top : top + ACQ_DEV, :] = mixed
 
 
 def acq_rows(recv_ref, part, r):

time: 65.2 us -> 65.1 us (level)
  no operation moved by 1% of the time
where the time goes in v9:
time: 65.1 us; the launch traced here: 64.5 us
  blocking collectives  50.2 us (77%)
  Pallas kernels  7.46 us (11%)
  starting transfers between devices  6.17 us (9%)
  between operations  0.7 us (1%)
    all_to_all x1, blocking collectives, per_device(): recv = lax.all_to_all(send, 'acq', split_axis=0, concat_axis=0, tiled=True)  36.6 us
    all_to_all x1, blocking collectives, per_device(): lax.all_to_all(result.reshape(DEVS, 2, 128), 'acq', split_axis=0, concat_...  13.5 us
    ppermute x1, starting transfers between devices, per_device(): chip = lax.ppermute(chip, 'az', across + [(j, i) for i, j in across])  6.07 us
    pallas_call x1, Pallas kernels, per_device(): call(own_kernel, OWN_OUTS, [VMEM], OWN_SCRATCH, cost_estimate=cost[0])(recv)  2.25 us
    pallas_call x1, Pallas kernels, per_device(): call(pack_kernel, f32(DEVS * CHUNK, 128), [HBM] * 3, (((ROWS, ACQ_DEV, RG...  1.68 us
    pallas_call x1, Pallas kernels, per_device(): call(chip_kernel, f32(2 * DEVS, 128), [VMEM] * 6, CHIP_SCRATCH)  1.54 us
  transfers between devices with their start and end apart: 2, of which 0 were waited for; matrix products, arithmetic and copies ran while one was open for 0% of the time, Pallas kernels for 5%

profile of v9, /device:TPU:1, one launch (start us, length us, event | category | flops | bytes accessed | tf_op | source)
XLA Modules:
  0.0 64.5 jit_solution(2821024934818012681)
XLA Ops:
  0.6 1.7 %shard_map.58 = f32[1920,128]{1,0:T(8,128)S(1)} custom-call(f32[10,6,1280]{2,1,0:T(8,128)} %bitcast.15, f32[10,6,1280]{2,1,0:T(8,128)} %bitcast.16, s32[2,16]{1,0:T(2,128)} %bitcast.17), custom_call_target="tpu_custom_call" | custom-call | tf_op jit(solution)/shard_map/pallas_call | solution.py:379
  2.3 36.6 %all_to_all.10 = f32[32,15,4,128]{3,2,1,0:T(4,128)S(1)} all-to-all(f32[32,15,4,128]{3,2,1,0:T(4,128)S(1)} %bitcast.12), channel_id=1, replica_groups=mesh['acq'=32,'az'=8] {'acq'}, dimensions={0} | all-to-all | bytes 1966080 | tf_op jit(solution)/shard_map/all_to_all | solution.py:394
  39.0 0.2 shard_map.59
  39.1 6.1 %collective-permute-start = (f32[392,128]{1,0:T(8,128)S(1)}, f32[392,128]{1,0:T(8,128)S(1)}, u32[]{:S(2)}, u32[]{:S(2)}) collective-permute-start(f32[392,128]{1,0:T(8,128)S(1)} %get-tuple-element.15), channel_id=1, source_target_pairs={{1,2},{3,4},{5,6},{2,1},{4,3},{6,5},{9,10},{11,12},{13,14},{10,9},... | collective-permute-start | bytes 602120 | tf_op jit(solution)/shard_map/ppermute | solution.py:400
  45.2 0.1 collective-permute-start.1
  45.3 2.3 %shard_map.60 = (f32[1024,256]{1,0:T(8,128)S(1)}, f32[1024,256]{1,0:T(8,128)S(1)}, f32[192,256]{1,0:T(8,128)S(1)}, f32[192,256]{1,0:T(8,128)S(1)}, bf16[512,256]...) custom-call(f32[1920,128]{1,0:T(8,128)S(1)} %bitcast.11), custom_call_target="tpu_custom_call" | custom-call | flops 1000 | bytes 1000 | tf_op jit(solution)/shard_map/pallas_call | solution.py:403
  47.6 0.0 collective-permute-done.1.core_ref
  47.6 1.1 %shard_map.61.value_ref = f32[512,128]{1,0:T(8,128)S(1)} custom-call(f32[384,128]{1,0:T(8,128)S(1)} %collective-permute-done.1.core_ref, f32[1024,256]{1,0:T(8,128)S(1)} %get-tuple-element.21.sums_ref, f32[192,256]{1,0:T(8,128)S(1)} %get-tuple-element.22.power_ref, bf16[512,256]{1,0:T(8,128)(2,1)S(1)} %get-tuple-element.18.pick_a, ...), custom_call_target="tpu_custom_call" | custom-call | flops 1000 | bytes 1000 | tf_op jit(solution)/shard_map/pallas_call | solution.py:405
  48.7 0.0 collective-permute-done.chip_ref
  48.7 1.5 %shard_map.62 = f32[64,128]{1,0:T(8,128)S(1)} custom-call(f32[392,128]{1,0:T(8,128)S(1)} %collective-permute-done.chip_ref, f32[1024,256]{1,0:T(8,128)S(1)} %get-tuple-element.16.sums_ref, f32[192,256]{1,0:T(8,128)S(1)} %get-tuple-element.17.power_ref, bf16[512,256]{1,0:T(8,128)(2,1)S(1)} %get-tuple-element.18.pick_a, ...), custom_call_target="tpu_custom_call" | custom-call | tf_op jit(solution)/shard_map/pallas_call | solution.py:408
  50.3 13.5 %all_to_all.11 = f32[32,2,128]{2,1,0:T(2,128)S(1)} all-to-all(f32[32,2,128]{2,1,0:T(2,128)S(1)} %bitcast.13), channel_id=1, replica_groups=mesh['acq'=32,'az'=8] {'acq'}, dimensions={0} | all-to-all | bytes 65536 | tf_op jit(solution)/shard_map/all_to_all | solution.py:411
  63.8 0.7 %shard_map.63 = (f32[32,64]{1,0:T(8,128)}, f32[32,64]{1,0:T(8,128)}, f32[32,64]{1,0:T(8,128)}) custom-call(f32[64,128]{1,0:T(8,128)S(1)} %bitcast.14), custom_call_target="tpu_custom_call" | custom-call | tf_op jit(solution)/shard_map/pallas_call | solution.py:412
Async XLA Ops:
  39.1 9.6 %collective-permute-start = (f32[392,128]{1,0:T(8,128)S(1)}, f32[392,128]{1,0:T(8,128)S(1)}, u32[]{:S(2)}, u32[]{:S(2)}) collective-permute-start(f32[392,128]{1,0:T(8,128)S(1)} %get-tuple-element.15), channel_id=1, source_target_pairs={{1,2},{3,4},{5,6},{2,1},{4,3},{6,5},{9,10},{11,12},{13,14},{10,9},... | collective-permute-start | bytes 602120 | tf_op jit(solution)/shard_map/ppermute | solution.py:400
  45.2 2.4 %collective-permute-start.1 = (f32[384,128]{1,0:T(8,128)S(1)}, f32[384,128]{1,0:T(8,128)S(1)}, u32[]{:S(2)}, u32[]{:S(2)}) collective-permute-start(f32[384,128]{1,0:T(8,128)S(1)} %get-tuple-element.20), channel_id=1, source_target_pairs={{0,1},{2,3},{4,5},{6,7},{1,0},{3,2},{5,4},{7,6},{8,9},{10,11},{12,... | collective-permute-start | bytes 589832 | tf_op jit(solution)/shard_map/ppermute | solution.py:401

commit v10 on v9

--- a/solution.py
+++ b/solution.py
@@ -100,14 +100,19 @@
     )
 
 
-def edges_kernel(recv_ref, chip_ref, core_ref):
+def chip_edge_kernel(recv_ref, out_ref):
     lane = lanes_of((ACQ, 128))
     for part in range(2):
-        v0, v1, v3, v4 = [acq_rows(recv_ref, part, r) for r in (0, 1, 3, 4)]
-        rows = slice(part * ACQ, (part + 1) * ACQ)
-        chip_ref[rows, :] = jnp.where(lane < 64, v0, pltpu.roll(v1, 64, 1))
-        core_ref[rows, :] = jnp.where(lane < 64, pltpu.roll(v3, 64, 1), v4)
-    chip_ref[2 * ACQ :, :] = jnp.zeros((8, 128), F32)
+        v0, v1 = [acq_rows(recv_ref, part, r) for r in (0, 1)]
+        out_ref[part * ACQ : (part + 1) * ACQ, :] = jnp.where(lane < 64, v0, pltpu.roll(v1, 64, 1))
+    out_ref[2 * ACQ :, :] = jnp.zeros((8, 128), F32)
+
+
+def core_edge_kernel(recv_ref, out_ref):
+    lane = lanes_of((ACQ, 128))
+    for part in range(2):
+        v3, v4 = [acq_rows(recv_ref, part, r) for r in (3, 4)]
+        out_ref[part * ACQ : (part + 1) * ACQ, :] = jnp.where(lane < 64, pltpu.roll(v3, 64, 1), v4)
 
 
 def pieces_of(x, count):
@@ -393,7 +398,8 @@
     send = send.reshape(DEVS, CHUNK // 4, 4, 128)
     recv = lax.all_to_all(send, "acq", split_axis=0, concat_axis=0, tiled=True)
     recv = recv.reshape(DEVS * CHUNK, 128)
-    chip, core = call(edges_kernel, (f32(2 * ACQ + 8, 128), f32(2 * ACQ, 128)), [VMEM])(recv)
+    chip = call(chip_edge_kernel, f32(2 * ACQ + 8, 128), [VMEM])(recv)
+    core = call(core_edge_kernel, f32(2 * ACQ, 128), [VMEM])(recv)
     count = lax.axis_size("az")
     across = [(i, i + 1) for i in range(1, count - 1, 2)]
     inside = [(i, i + 1) for i in range(0, count, 2)]

time: 65.1 us -> 65.1 us (level)
  no operation moved by 1% of the time
where the time goes in v10:
time: 65.1 us; the launch traced here: 64.6 us
  blocking collectives  50.2 us (77%)
  Pallas kernels  7.52 us (12%)
  starting transfers between devices  6.17 us (9%)
  between operations  0.7 us (1%)
    all_to_all x1, blocking collectives, per_device(): recv = lax.all_to_all(send, 'acq', split_axis=0, concat_axis=0, tiled=True)  36.6 us
    all_to_all x1, blocking collectives, per_device(): lax.all_to_all(result.reshape(DEVS, 2, 128), 'acq', split_axis=0, concat_...  13.5 us
    ppermute x1, starting transfers between devices, per_device(): chip = lax.ppermute(chip, 'az', across + [(j, i) for i, j in across])  6.07 us
    pallas_call x1, Pallas kernels, per_device(): call(own_kernel, OWN_OUTS, [VMEM], OWN_SCRATCH, cost_estimate=cost[0])(recv)  2.25 us
    pallas_call x1, Pallas kernels, per_device(): call(pack_kernel, f32(DEVS * CHUNK, 128), [HBM] * 3, (((ROWS, ACQ_DEV, RG...  1.68 us
    pallas_call x1, Pallas kernels, per_device(): call(chip_kernel, f32(2 * DEVS, 128), [VMEM] * 6, CHIP_SCRATCH)  1.54 us
  transfers between devices with their start and end apart: 2, of which 0 were waited for; matrix products, arithmetic and copies ran while one was open for 0% of the time, Pallas kernels for 5%

profile of v10, /device:TPU:1, one launch (start us, length us, event | category | flops | bytes accessed | tf_op | source)
XLA Modules:
  0.0 64.6 jit_solution(15362416649869861492)
XLA Ops:
  0.6 1.7 %shard_map.58 = f32[1920,128]{1,0:T(8,128)S(1)} custom-call(f32[10,6,1280]{2,1,0:T(8,128)} %bitcast.16, f32[10,6,1280]{2,1,0:T(8,128)} %bitcast.17, s32[2,16]{1,0:T(2,128)} %bitcast.18), custom_call_target="tpu_custom_call" | custom-call | tf_op jit(solution)/shard_map/pallas_call | solution.py:384
  2.3 36.6 %all_to_all.10 = f32[32,15,4,128]{3,2,1,0:T(4,128)S(1)} all-to-all(f32[32,15,4,128]{3,2,1,0:T(4,128)S(1)} %bitcast.13), channel_id=1, replica_groups=mesh['acq'=32,'az'=8] {'acq'}, dimensions={0} | all-to-all | bytes 1966080 | tf_op jit(solution)/shard_map/all_to_all | solution.py:399
  39.0 0.1 shard_map.59
  39.1 6.1 %collective-permute-start = (f32[392,128]{1,0:T(8,128)S(1)}, f32[392,128]{1,0:T(8,128)S(1)}, u32[]{:S(2)}, u32[]{:S(2)}) collective-permute-start(f32[392,128]{1,0:T(8,128)S(1)} %shard_map.59), channel_id=1, source_target_pairs={{1,2},{3,4},{5,6},{2,1},{4,3},{6,5},{9,10},{11,12},{13,14},{10,9},... | collective-permute-start | bytes 602120 | tf_op jit(solution)/shard_map/ppermute | solution.py:406
  45.2 0.1 shard_map.61
  45.3 0.1 collective-permute-start.1
  45.4 2.3 %shard_map.60 = (f32[1024,256]{1,0:T(8,128)S(1)}, f32[1024,256]{1,0:T(8,128)S(1)}, f32[192,256]{1,0:T(8,128)S(1)}, f32[192,256]{1,0:T(8,128)S(1)}, bf16[512,256]...) custom-call(f32[1920,128]{1,0:T(8,128)S(1)} %bitcast.12), custom_call_target="tpu_custom_call" | custom-call | flops 1000 | bytes 1000 | tf_op jit(solution)/shard_map/pallas_call | solution.py:409
  47.6 0.0 collective-permute-done.1.core_ref
  47.6 1.1 %shard_map.62.value_ref = f32[512,128]{1,0:T(8,128)S(1)} custom-call(f32[384,128]{1,0:T(8,128)S(1)} %collective-permute-done.1.core_ref, f32[1024,256]{1,0:T(8,128)S(1)} %get-tuple-element.17.sums_ref, f32[192,256]{1,0:T(8,128)S(1)} %get-tuple-element.18.power_ref, bf16[512,256]{1,0:T(8,128)(2,1)S(1)} %get-tuple-element.15.pick_a, ...), custom_call_target="tpu_custom_call" | custom-call | flops 1000 | bytes 1000 | tf_op jit(solution)/shard_map/pallas_call | solution.py:411
  48.8 0.0 collective-permute-done.chip_ref
  48.8 1.5 %shard_map.63 = f32[64,128]{1,0:T(8,128)S(1)} custom-call(f32[392,128]{1,0:T(8,128)S(1)} %collective-permute-done.chip_ref, f32[1024,256]{1,0:T(8,128)S(1)} %get-tuple-element.13.sums_ref, f32[192,256]{1,0:T(8,128)S(1)} %get-tuple-element.14.power_ref, bf16[512,256]{1,0:T(8,128)(2,1)S(1)} %get-tuple-element.15.pick_a, ...), custom_call_target="tpu_custom_call" | custom-call | tf_op jit(solution)/shard_map/pallas_call | solution.py:414
  50.3 13.5 %all_to_all.11 = f32[32,2,128]{2,1,0:T(2,128)S(1)} all-to-all(f32[32,2,128]{2,1,0:T(2,128)S(1)} %bitcast.14), channel_id=1, replica_groups=mesh['acq'=32,'az'=8] {'acq'}, dimensions={0} | all-to-all | bytes 65536 | tf_op jit(solution)/shard_map/all_to_all | solution.py:417
  63.9 0.7 %shard_map.64 = (f32[32,64]{1,0:T(8,128)}, f32[32,64]{1,0:T(8,128)}, f32[32,64]{1,0:T(8,128)}) custom-call(f32[64,128]{1,0:T(8,128)S(1)} %bitcast.15), custom_call_target="tpu_custom_call" | custom-call | tf_op jit(solution)/shard_map/pallas_call | solution.py:418
Async XLA Ops:
  39.1 9.7 %collective-permute-start = (f32[392,128]{1,0:T(8,128)S(1)}, f32[392,128]{1,0:T(8,128)S(1)}, u32[]{:S(2)}, u32[]{:S(2)}) collective-permute-start(f32[392,128]{1,0:T(8,128)S(1)} %shard_map.59), channel_id=1, source_target_pairs={{1,2},{3,4},{5,6},{2,1},{4,3},{6,5},{9,10},{11,12},{13,14},{10,9},... | collective-permute-start | bytes 602120 | tf_op jit(solution)/shard_map/ppermute | solution.py:406
  45.3 2.4 %collective-permute-start.1 = (f32[384,128]{1,0:T(8,128)S(1)}, f32[384,128]{1,0:T(8,128)S(1)}, u32[]{:S(2)}, u32[]{:S(2)}) collective-permute-start(f32[384,128]{1,0:T(8,128)S(1)} %shard_map.61), channel_id=1, source_target_pairs={{0,1},{2,3},{4,5},{6,7},{1,0},{3,2},{5,4},{7,6},{8,9},{10,11},{12,... | collective-permute-start | bytes 589832 | tf_op jit(solution)/shard_map/ppermute | solution.py:407
